TPU v7x, 512 devices: a whole 4x8x8 slice. The times are simulated.
512 devices in a mesh: blk: 128 (over x, z, y_hi, core), feat: 4 (over y_lo).
Axes of the slice: x: 4, y: 8 (y_hi: 2, y_lo: 4; y = y_hi * 4 + y_lo), z: 8, core: 2. Of those that a mesh axis runs over, the one named last changes fastest.
Arguments:
- features: bfloat16 [256, 32768], P('feat', 'blk'), may hold values from -6 to 6
- near_tiles: bfloat16 [32768, 7, 256], P('blk'), may hold values from 0 to 1
- far_tiles: bfloat16 [12288, 128, 128], P('blk'), may hold values from 0 to 1
- far_source: int32 [12288, 1], P('blk'), may hold values from 0 to 127; in each aligned block of 96 rows (0 to 95, 96 to 191, ...) at most 2 rows name the same one
- far_index: int32 [12288, 2], P('blk'), may hold values from 0 to 1
- weight: bfloat16 [256, 256], P(None, 'feat'), may hold values from -0.375 to 0.375
- bias: float32 [256], P('feat'), may hold values from -3 to 3
- grad_out: bfloat16 [256, 32768], P('feat', 'blk'), may hold values from -6 to 6
Outputs:
- activated: bfloat16 [256, 32768], P('feat', 'blk')
- grad_feat: bfloat16 [256, 32768], P('feat', 'blk')
- grad_weight: float32 [256, 256], P(None, 'feat')
- grad_bias: float32 [256], P('feat')
Inputs may be any that keep to these rules, and one draw needn't show every extreme that they name: `far_source`: in the 96 rows of one row block no value appears more than 2 times, and some value appears exactly 2 times.
All inputs are finite; a program needn't handle non-finite values.
Results may differ from a plain program's by a relative error of at most 0.01.
Values may be sent and summed in bfloat16 or wider, within the bound.
A program may use at most 64 MiB of HBM per device.

v0:
```python
import jax
import jax.numpy as jnp
from jax import lax
from jax.sharding import PartitionSpec as P

MOST = 2


def shifted(block, axis, distance):
    devices = range(lax.axis_size(axis))
    route = [((i - distance) % len(devices), i) for i in devices]
    return lax.ppermute(block, axis, route)


def on_device(features, near_tiles, far_tiles, far_source, far_index, weight, bias, grad_out):
    hidden_dev, row_total = features.shape
    far_count, tile_size = (far_tiles.shape[0], far_tiles.shape[1])
    tile_count = row_total // tile_size
    blocks = lax.axis_size("blk")
    pieces = []
    for offset in (-3, -2, -1, 0, 1, 2, 3):
        if offset == 0:
            pieces.append(features)
        else:
            pieces.append(shifted(features, "blk", -offset))
    stacked = jnp.stack(pieces, axis=1)
    near_sum = jnp.einsum("hsb,asb->ha", stacked, near_tiles, preferred_element_type=jnp.float32)
    source = far_source[:, 0]
    own_tile = far_index[:, 0]
    src_tile = far_index[:, 1]
    tile_order = jnp.arange(far_count, dtype=jnp.int32)
    same_source = source[:, None] == source[None, :]
    earlier = tile_order[None, :] < tile_order[:, None]
    slot_rank = jnp.sum((same_source & earlier).astype(jnp.int32), axis=1)
    slot_index = source * MOST + slot_rank
    requests = (
        jnp.full((blocks * MOST,), -1, jnp.int32).at[slot_index].set(src_tile).reshape(blocks, MOST)
    )
    wanted = lax.all_to_all(requests, "blk", split_axis=0, concat_axis=0, tiled=True)
    tiles_rows = jnp.transpose(features.reshape(hidden_dev, tile_count, tile_size), (1, 0, 2))
    picked = jnp.take(tiles_rows, jnp.maximum(wanted, 0), axis=0)
    outgoing = jnp.where((wanted >= 0)[:, :, None, None], picked, jnp.zeros_like(picked))
    arrived = lax.all_to_all(outgoing, "blk", split_axis=0, concat_axis=0, tiled=True)
    far_inputs = jnp.take(arrived.reshape(blocks * MOST, hidden_dev, tile_size), slot_index, axis=0)
    partial_value = jnp.einsum(
        "khb,kab->kha", far_inputs, far_tiles, preferred_element_type=jnp.float32
    )
    far_sum = (
        jnp.zeros((tile_count, hidden_dev, tile_size), jnp.float32).at[own_tile].add(partial_value)
    )
    aggregated = (
        near_sum + jnp.transpose(far_sum, (1, 0, 2)).reshape(hidden_dev, row_total)
    ).astype(jnp.bfloat16)
    gathered = lax.all_gather(aggregated, "feat", axis=0, tiled=True)
    pre_act = (
        jnp.einsum("io,ia->oa", weight, gathered, preferred_element_type=jnp.float32)
        + bias[:, None]
    )
    activated = jax.nn.silu(pre_act).astype(jnp.bfloat16)
    sigmoid_pre = jax.nn.sigmoid(pre_act)
    grad_pre = (
        grad_out.astype(jnp.float32) * sigmoid_pre * (1.0 + pre_act * (1.0 - sigmoid_pre))
    ).astype(jnp.bfloat16)
    weight_part = jnp.einsum("ia,oa->io", gathered, grad_pre, preferred_element_type=jnp.float32)
    bias_part = jnp.sum(grad_pre.astype(jnp.float32), axis=1)
    grad_weight, grad_bias = lax.psum((weight_part, bias_part), "blk")
    grad_agg = lax.psum_scatter(
        jnp.dot(weight, grad_pre, preferred_element_type=jnp.float32),
        "feat",
        scatter_dimension=0,
        tiled=True,
    ).astype(jnp.bfloat16)
    band_parts = jnp.einsum("ha,asb->shb", grad_agg, near_tiles, preferred_element_type=jnp.float32)
    band_total = band_parts[3]
    for offset in (-3, -2, -1, 1, 2, 3):
        band_total = band_total + shifted(
            band_parts[offset + 3].astype(jnp.bfloat16), "blk", offset
        ).astype(jnp.float32)
    chosen = jnp.take(grad_agg.reshape(hidden_dev, tile_count, tile_size), own_tile, axis=1)
    far_partial = jnp.einsum(
        "hka,kab->khb", chosen, far_tiles, preferred_element_type=jnp.float32
    ).astype(jnp.bfloat16)
    outgoing_grads = (
        jnp.zeros((blocks * MOST, hidden_dev, tile_size), jnp.bfloat16)
        .at[slot_index]
        .set(far_partial)
    )
    returned = lax.all_to_all(
        outgoing_grads.reshape(blocks, MOST, hidden_dev, tile_size),
        "blk",
        split_axis=0,
        concat_axis=0,
        tiled=True,
    )
    match_table = (
        wanted.reshape(-1)[:, None] == jnp.arange(tile_count, dtype=jnp.int32)[None, :]
    ).astype(jnp.bfloat16)
    far_total = jnp.einsum(
        "shb,st->thb",
        returned.reshape(blocks * MOST, hidden_dev, tile_size),
        match_table,
        preferred_element_type=jnp.float32,
    )
    grad_feat = (
        band_total + jnp.transpose(far_total, (1, 0, 2)).reshape(hidden_dev, row_total)
    ).astype(jnp.bfloat16)
    return (activated, grad_feat, grad_weight, grad_bias)


def solution(mesh):
    return jax.shard_map(
        on_device,
        mesh=mesh,
        in_specs=(
            P("feat", "blk"),
            P("blk", None, None),
            P("blk", None, None),
            P("blk", None),
            P("blk", None),
            P(None, "feat"),
            P("feat"),
            P("feat", "blk"),
        ),
        out_specs=(P("feat", "blk"), P("feat", "blk"), P(None, "feat"), P("feat")),
        check_vma=False,
    )
```

profile of v0, /device:TPU:1, one launch (start us, length us, event | category | flops | bytes accessed | tf_op | source)
XLA Modules:
  0.0 1715.8 jit_solution(12452386812584246228)
XLA Ops:
  8.0 1.0 convert_reduce_fusion.1
  9.0 0.7 and_bitcast_fusion.1
  9.7 0.8 slice_bitcast_fusion.7
  10.4 0.9 scatter_custom_fusion
  11.3 0.8 all_to_all.12
  12.1 20.9 %all-to-all-start = ((s32[128,1,2]{2,1,0:T(1,128)}), s32[128,1,2]{2,1,0:T(1,128)S(1)}, u32[]{:S(2)}, u32[]{:S(2)}) async-start(s32[128,1,2]{2,1,0:T(1,128)} %bitcast.14), calls=%async_computation | async-start | bytes 131072 | tf_op jit(solution)/shard_map/all_to_all | solution.py:39
  33.0 0.8 bitcast_bitcast_fusion
  33.8 13.6 all-to-all-done
  47.3 0.1 copy.53
  47.4 0.1 copy.54
  47.5 0.1 copy.56
  47.7 0.1 copy.58
  47.8 0.1 reshape.91
  48.0 3.0 gather_fusion
  51.0 3.9 select_select_fusion
  54.9 7.1 all-to-all-start.1
  62.0 3.6 collective-permute-start
  65.6 7.0 collective-permute-start.1
  72.6 7.3 collective-permute-start.2
  80.0 1.9 collective-permute-start.3
  81.9 6.4 collective-permute-start.4
  88.3 72.4 %collective-permute-done = bf16[64,256]{1,0:T(8,128)(2,1)S(1)} collective-permute-done((bf16[64,256]{1,0:T(8,128)(2,1)S(1)}, bf16[64,256]{1,0:T(8,128)(2,1)S(1)}, u32[]{:S(2)}, u32[]{:S(2)}) %collective-permute-start) | collective-permute-done | bytes 32800 | tf_op jit(solution)/shard_map/ppermute | solution.py:12
  160.7 6.3 collective-permute-start.5
  167.0 0.6 bitcast_dynamic-update-slice_fusion.6
  167.7 0.6 bitcast_dynamic-update-slice_fusion.5
  168.3 0.6 bitcast_dynamic-update-slice_fusion.4
  168.9 0.6 bitcast_dynamic-update-slice_fusion.3
  169.5 0.6 bitcast_dynamic-update-slice_fusion.2
  170.1 0.6 bitcast_dynamic-update-slice_fusion.1
  170.8 0.6 bitcast_dynamic-update-slice_fusion
  171.4 4.2 gather_fusion.1
  175.6 5.3 fusion.2
  180.9 10.3 scatter_fusion
  191.2 1.7 fusion.8
  193.0 12.2 all_gather.3
  205.2 0.9 convert_reduce_fusion
  206.1 0.2 convolution_bitcast_fusion.1
  206.3 0.8 copy.64
  207.2 24.3 %reduce-scatter.4.cloned.1.call-done = f32[64,256]{1,0:T(8,128)} async-done(((f32[256,256]{1,0:T(8,128)}), f32[64,256]{1,0:T(8,128)}) %reduce-scatter.4.cloned.1.call-update) | async-done | bytes 65552 | tf_op jit(solution)/shard_map/reduce_scatter | solution.py:67
  231.5 0.8 copy_bitcast_fusion
  232.3 2.0 gather_fusion.2
  234.3 3.6 convolution_convert_fusion
  237.9 3.0 broadcast_in_dim.66
  240.9 13.4 scatter_fusion.1
  254.3 12.6 copy.62
  266.9 16.5 all-to-all-start.2
  283.4 0.0 all-reduce.2.cloned.1.call-start
  283.4 0.5 broadcast.104
  283.9 0.8 reduce.3
  284.7 0.1 eq.34
  284.9 2.3 fusion.31
  287.2 7.2 collective-permute-start.10
  294.4 0.8 fusion.32
  295.2 479.4 %psum.15 = f32[64]{0:T(128)} all-reduce(f32[64]{0:T(128)S(1)} %get-tuple-element.4), channel_id=1, replica_groups=mesh['blk'=128,'feat'=4] {'blk'}, use_global_device_ids=true, to_apply=%region_7.8 | all-reduce | flops 64 | bytes 512 | tf_op jit(solution)/shard_map/psum | solution.py:66
  774.7 1.9 collective-permute-start.11
  776.6 11.8 collective-permute-start.6
  788.4 1.9 collective-permute-start.7
  790.3 2.3 collective-permute-start.8
  792.6 8.8 copy.63
  801.4 7.2 collective-permute-start.9
  808.6 2.8 fusion.21
  811.4 1.5 fusion.11
  812.9 894.0 %all-reduce.2.cloned.1.call-done = f32[256,64]{0,1:T(8,128)} async-done(((f32[256,64]{0,1:T(8,128)}), f32[256,64]{0,1:T(8,128)}) %all-reduce.2.cloned.1.call-update) | async-done | bytes 65552 | tf_op jit(solution)/shard_map/psum | solution.py:66
  1706.9 1.5 copy.83
  (42 shorter events, 0.2 us)
Async XLA Ops:
  8.0 167.6 %copy-start = (bf16[96,128,128]{2,1,0:T(8,128)(2,1)S(1)}, bf16[96,128,128]{2,1,0:T(8,128)(2,1)}, u32[]{:S(2)}) copy-start(bf16[96,128,128]{2,1,0:T(8,128)(2,1)} %param.10) | copy-start | bytes 9437188
  12.1 35.2 %all-to-all-start = ((s32[128,1,2]{2,1,0:T(1,128)}), s32[128,1,2]{2,1,0:T(1,128)S(1)}, u32[]{:S(2)}, u32[]{:S(2)}) async-start(s32[128,1,2]{2,1,0:T(1,128)} %bitcast.14), calls=%async_computation | async-start | bytes 131072 | tf_op jit(solution)/shard_map/all_to_all | solution.py:39
  54.9 7.1 copy-start.4
  54.9 116.5 %all-to-all-start.1 = ((bf16[128,2,64,128]{3,2,1,0:T(8,128)(2,1)}), bf16[128,2,64,128]{3,2,1,0:T(8,128)(2,1)}, u32[]{:S(2)}, u32[]{:S(2)}) async-start(bf16[128,2,64,128]{3,2,1,0:T(8,128)(2,1)} %select_select_fusion), calls=%async_computation.1 | async-start | bytes 8388608 | tf_op jit(solution)/shard_map/all_to_all | solution.py:43
  62.0 169.5 %reduce-scatter.4.cloned.1.call-start = ((), (), s32[]{:S(2)}) async-start(), calls=%async_computation.5 | async-start | bytes 327680 | tf_op jit(solution)/shard_map/reduce_scatter | solution.py:67
  62.0 98.7 %collective-permute-start = (bf16[64,256]{1,0:T(8,128)(2,1)S(1)}, bf16[64,256]{1,0:T(8,128)(2,1)S(1)}, u32[]{:S(2)}, u32[]{:S(2)}) collective-permute-start(bf16[64,256]{1,0:T(8,128)(2,1)S(1)} %copy-done.4), channel_id=1, source_target_pairs={{500,0},{504,4},{508,8},{0,12},{4,16},{8,20},{12,24},{16,28},{20,3... | collective-permute-start | bytes 98312 | tf_op jit(solution)/shard_map/ppermute | solution.py:12
  65.6 102.1 %collective-permute-start.1 = (bf16[64,256]{1,0:T(8,128)(2,1)S(1)}, bf16[64,256]{1,0:T(8,128)(2,1)S(1)}, u32[]{:S(2)}, u32[]{:S(2)}) collective-permute-start(bf16[64,256]{1,0:T(8,128)(2,1)S(1)} %copy-done.4), channel_id=1, source_target_pairs={{504,0},{508,4},{0,8},{4,12},{8,16},{12,20},{16,24},{20,28},{24,32... | collective-permute-start | bytes 98312 | tf_op jit(solution)/shard_map/ppermute | solution.py:12
  72.6 95.7 %collective-permute-start.2 = (bf16[64,256]{1,0:T(8,128)(2,1)S(1)}, bf16[64,256]{1,0:T(8,128)(2,1)S(1)}, u32[]{:S(2)}, u32[]{:S(2)}) collective-permute-start(bf16[64,256]{1,0:T(8,128)(2,1)S(1)} %copy-done.4), channel_id=1, source_target_pairs={{508,0},{0,4},{4,8},{8,12},{12,16},{16,20},{20,24},{24,28},{28,32}... | collective-permute-start | bytes 98312 | tf_op jit(solution)/shard_map/ppermute | solution.py:12
  80.0 89.6 %collective-permute-start.3 = (bf16[64,256]{1,0:T(8,128)(2,1)S(1)}, bf16[64,256]{1,0:T(8,128)(2,1)S(1)}, u32[]{:S(2)}, u32[]{:S(2)}) collective-permute-start(bf16[64,256]{1,0:T(8,128)(2,1)S(1)} %copy-done.4), channel_id=1, source_target_pairs={{4,0},{8,4},{12,8},{16,12},{20,16},{24,20},{28,24},{32,28},{36,32}... | collective-permute-start | bytes 98312 | tf_op jit(solution)/shard_map/ppermute | solution.py:12
  81.9 88.3 %collective-permute-start.4 = (bf16[64,256]{1,0:T(8,128)(2,1)S(1)}, bf16[64,256]{1,0:T(8,128)(2,1)S(1)}, u32[]{:S(2)}, u32[]{:S(2)}) collective-permute-start(bf16[64,256]{1,0:T(8,128)(2,1)S(1)} %copy-done.4), channel_id=1, source_target_pairs={{8,0},{12,4},{16,8},{20,12},{24,16},{28,20},{32,24},{36,28},{40,32... | collective-permute-start | bytes 98312 | tf_op jit(solution)/shard_map/ppermute | solution.py:12
  160.7 10.1 collective-permute-start.5
  180.8 24.3 %copy-start.5 = (bf16[256,64]{0,1:T(8,128)(2,1)S(1)}, bf16[256,64]{0,1:T(8,128)(2,1)}, u32[]{:S(2)}) copy-start(bf16[256,64]{0,1:T(8,128)(2,1)} %param.13) | copy-start | bytes 98308
  180.9 24.3 %copy-start.7 = (bf16[64,256]{1,0:T(8,128)(2,1)S(1)}, bf16[64,256]{1,0:T(8,128)(2,1)}, u32[]{:S(2)}) copy-start(bf16[64,256]{1,0:T(8,128)(2,1)} %param.15) | copy-start | bytes 98308
  180.9 24.3 %copy-start.8 = (f32[64]{0:T(128)S(1)}, f32[64]{0:T(128)}, u32[]{:S(2)}) copy-start(f32[64]{0:T(128)} %param.14) | copy-start | bytes 772
  180.9 26.3 %copy-start.6 = (s32[96,2]{0,1:T(2,128)S(1)}, s32[96,2]{0,1:T(2,128)}, u32[]{:S(2)}) copy-start(s32[96,2]{0,1:T(2,128)} %param.12) | copy-start | bytes 2308
  205.1 0.9 copy-start.1
  266.9 18.0 %copy-start.3 = (f32[64,256]{1,0:T(8,128)S(1)}, f32[64,256]{1,0:T(8,128)}, u32[]{:S(2)}) copy-start(f32[64,256]{1,0:T(8,128)} %reduce-scatter.4.cloned.1.call-done) | copy-start | bytes 196612
  266.9 27.5 %copy-start.2 = (bf16[256,256]{1,0:T(8,128)(2,1)S(1)}, bf16[256,256]{1,0:T(8,128)(2,1)}, u32[]{:S(2)}) copy-start(bf16[256,256]{1,0:T(8,128)(2,1)} %copy-done.1) | copy-start | bytes 393220
  266.9 525.7 %all-to-all-start.2 = ((bf16[128,2,64,128]{3,1,2,0:T(2,128)(2,1)}), bf16[128,2,64,128]{3,1,2,0:T(2,128)(2,1)}, u32[]{:S(2)}, u32[]{:S(2)}) async-start(bf16[128,2,64,128]{3,1,2,0:T(2,128)(2,1)} %copy.62), calls=%async_computation.2 | async-start | bytes 8388608 | tf_op jit(solution)/shard_map/all_to_all | solution.py:88
  283.4 1423.6 %all-reduce.2.cloned.1.call-start = ((), (), s32[]{:S(2)}) async-start(), calls=%async_computation.4 | async-start | bytes 131072 | tf_op jit(solution)/shard_map/psum | solution.py:66
  287.2 514.2 %collective-permute-start.10 = (bf16[64,256]{1,0:T(8,128)(2,1)S(1)}, bf16[64,256]{1,0:T(8,128)(2,1)S(1)}, u32[]{:S(2)}, u32[]{:S(2)}) collective-permute-start(bf16[64,256]{1,0:T(8,128)(2,1)S(1)} %get-tuple-element.10), channel_id=1, source_target_pairs={{504,0},{508,4},{0,8},{4,12},{8,16},{12,20},{16,24},{20,28},{24,32... | collective-permute-start | bytes 98312 | tf_op jit(solution)/shard_map/ppermute | solution.py:12
  774.7 36.7 %collective-permute-start.11 = (bf16[64,256]{1,0:T(8,128)(2,1)S(1)}, bf16[64,256]{1,0:T(8,128)(2,1)S(1)}, u32[]{:S(2)}, u32[]{:S(2)}) collective-permute-start(bf16[64,256]{1,0:T(8,128)(2,1)S(1)} %get-tuple-element.9), channel_id=1, source_target_pairs={{500,0},{504,4},{508,8},{0,12},{4,16},{8,20},{12,24},{16,28},{20,3... | collective-permute-start | bytes 98312 | tf_op jit(solution)/shard_map/ppermute | solution.py:12
  776.6 34.8 %collective-permute-start.6 = (bf16[64,256]{1,0:T(8,128)(2,1)S(1)}, bf16[64,256]{1,0:T(8,128)(2,1)S(1)}, u32[]{:S(2)}, u32[]{:S(2)}) collective-permute-start(bf16[64,256]{1,0:T(8,128)(2,1)S(1)} %get-tuple-element.8), channel_id=1, source_target_pairs={{12,0},{16,4},{20,8},{24,12},{28,16},{32,20},{36,24},{40,28},{44,3... | collective-permute-start | bytes 98312 | tf_op jit(solution)/shard_map/ppermute | solution.py:12
  788.4 23.0 %collective-permute-start.7 = (bf16[64,256]{1,0:T(8,128)(2,1)S(1)}, bf16[64,256]{1,0:T(8,128)(2,1)S(1)}, u32[]{:S(2)}, u32[]{:S(2)}) collective-permute-start(bf16[64,256]{1,0:T(8,128)(2,1)S(1)} %get-tuple-element.13), channel_id=1, source_target_pairs={{8,0},{12,4},{16,8},{20,12},{24,16},{28,20},{32,24},{36,28},{40,32... | collective-permute-start | bytes 98312 | tf_op jit(solution)/shard_map/ppermute | solution.py:12
  790.3 21.1 %collective-permute-start.8 = (bf16[64,256]{1,0:T(8,128)(2,1)S(1)}, bf16[64,256]{1,0:T(8,128)(2,1)S(1)}, u32[]{:S(2)}, u32[]{:S(2)}) collective-permute-start(bf16[64,256]{1,0:T(8,128)(2,1)S(1)} %get-tuple-element.12), channel_id=1, source_target_pairs={{4,0},{8,4},{12,8},{16,12},{20,16},{24,20},{28,24},{32,28},{36,32}... | collective-permute-start | bytes 98312 | tf_op jit(solution)/shard_map/ppermute | solution.py:12
  801.4 10.0 collective-permute-start.9
Sparse Core Ops, SparseCore 0:
  207.3 24.1 reduce-scatter.3
Sparse Core Ops, SparseCore 1:
  295.3 1411.5 all-reduce.1
where the time goes:
time: 1720 us
  waiting for transfers between devices  1000 us (58%)
  blocking collectives  492 us (29%)
  starting transfers between devices  109 us (6%)
  local copies, waits for them, and re-layouts  57.3 us (3%)
  other arithmetic  19.9 us (1%)
  matrix products  17.6 us (1%)
    psum x1, waiting for transfers between devices, on_device(): grad_weight, grad_bias = lax.psum((weight_part, bias_part), 'blk')  894 us
    psum x1, blocking collectives, on_device(): grad_weight, grad_bias = lax.psum((weight_part, bias_part), 'blk')  479 us
    ppermute x12, waiting for transfers between devices, shifted(): return lax.ppermute(block, axis, route)  72.4 us
    ppermute x12, starting transfers between devices, shifted(): return lax.ppermute(block, axis, route)  64.8 us
  transfers between devices with their start and end apart: 17, of which 4 were waited for; matrix products, arithmetic and copies ran while one was open for 1% of the time, Pallas kernels for 0%

commit v1 on v0

v1 whole, which is shorter than its diff:
```python
import functools

import jax
import jax.numpy as jnp
from jax import lax
from jax.experimental import pallas as pl
from jax.experimental.pallas import tpu as pltpu
from jax.sharding import PartitionSpec as P

NX, NZ, NY, NC = 4, 8, 2, 2
NB = NX * NZ * NY * NC
HALF = NB // NC
GROUP = NX * NY
FAR = 96
BAND = 7
NF = 4
HD = 64
TILE = 128
ROWS = 256
F32 = jnp.float32
BF16 = jnp.bfloat16
NN = (((1,), (0,)), ((), ()))
NT = (((1,), (1,)), ((), ()))
TN = (((0,), (0,)), ((), ()))
STEPS = (4, 3, -3, 2, -2, 1, -1, 0)


def dot(a, b, dims):
    return lax.dot_general(a, b, dims, preferred_element_type=F32)


def send(src, dst, sent, got, **where):
    return pltpu.make_async_remote_copy(
        src_ref=src, dst_ref=dst, send_sem=sent, recv_sem=got,
        device_id=where, device_id_type=pl.DeviceIdType.MESH,
    )


def rem(a, n):
    return lax.rem(a, jnp.int32(n))


def gather_blocks(own, X, me, sy, ry, sR, rR, sL, rL, sX, rX, sP, rP):
    x, z, y, core, at = me
    X[core * HALF + z * GROUP + x * NY + y] = own

    right, left = at(x, rem(z + 1, NZ), y, core), at(x, rem(z + NZ - 1, NZ), y, core)
    partner = at(x, z, y, 1 - core)
    mine = X.at[core * HALF + z * GROUP + x * NY + y]
    other = X.at[core * HALF + z * GROUP + x * NY + 1 - y]
    swap = send(mine, mine, sy, ry, blk=at(x, z, 1 - y, core))
    swap.start()
    send(other, other, sy, ry, blk=at(x, z, 1 - y, core)).wait_recv()

    def piece(k, xx, zz):
        return X.at[pl.ds(k * HALF + zz * GROUP + xx * NY, NY)]

    def part(k, xx, zz, yy):
        return X.at[pl.ds(k * HALF + zz * GROUP + xx * NY + yy, 1)]

    def to_partner(ref):
        send(ref, ref, sP, rP, blk=partner).start()

    def ring_step(k, xx, i, s, start):
        zr, zl = rem(z + NZ - s, NZ), rem(z + s, NZ)
        for zz, sem_s, sem_r, to, yy in ((zr, sR, rR, right, 0), (zl, sL, rL, left, 1)):
            if s > 0:
                ref = piece(k, xx, zz) if s < 4 else part(k, xx, zz, yy)
                send(ref, ref, sem_s.at[i, s - 1], sem_r.at[i, s - 1], blk=to).wait_recv()
            if s < 4:
                ref = piece(k, xx, zz) if s < 3 else part(k, xx, zz, yy)
                send(ref, ref, sem_s.at[i, s], sem_r.at[i, s], blk=to).start()

    def ring_sent(k, xx, i):
        for s in range(4):
            zr, zl = rem(z + NZ - s, NZ), rem(z + s, NZ)
            for zz, sem_s, sem_r, to, yy in ((zr, sR, rR, right, 0), (zl, sL, rL, left, 1)):
                ref = piece(k, xx, zz) if s < 3 else part(k, xx, zz, yy)
                send(ref, ref, sem_s.at[i, s], sem_r.at[i, s], blk=to).wait_send()

    def x_peer(d):
        return at(rem(x + d, NX), z, y, core)

    @pl.when(core == 0)
    def _():
        def spread(zz, j):
            ref = piece(0, x, zz)
            for d in (1, 3, 2):
                send(ref, ref, sX.at[d - 1, j], rX.at[d - 1, j], blk=x_peer(d)).start()
            to_partner(ref)

        def collect(zz, j):
            for d in (1, 3, 2):
                ref = piece(0, rem(x + NX - d, NX), zz)
                send(ref, ref, sX.at[d - 1, j], rX.at[d - 1, j], blk=x_peer(d)).wait_recv()
                to_partner(ref)

        places = [z] + [rem(z + o, NZ) for s in (1, 2, 3) for o in (NZ - s, s)] + [rem(z + 4, NZ)]
        steps = [[0], [1, 2], [3, 4], [5, 6], [7]]
        for s in range(5):
            ring_step(0, x, 0, s, None)
            for j in steps[s]:
                spread(places[j], j)
            if s > 0:
                for j in steps[s - 1]:
                    collect(places[j], j)
        collect(places[7], 7)
        ring_sent(0, x, 0)
        for j in range(8):
            for d in (1, 3, 2):
                ref = piece(0, x, places[j])
                send(ref, ref, sX.at[d - 1, j], rX.at[d - 1, j], blk=x_peer(d)).wait_send()

    @pl.when(core == 1)
    def _():
        ref = piece(1, x, z)
        for d in (1, 3, 2):
            send(ref, ref, sX.at[d - 1, 0], rX.at[d - 1, 0], blk=x_peer(d)).start()
        ring_step(1, x, 0, 0, None)
        to_partner(ref)
        for d in (1, 3, 2):
            xx = rem(x + NX - d, NX)
            got = piece(1, xx, z)
            send(got, got, sX.at[d - 1, 0], rX.at[d - 1, 0], blk=x_peer(d)).wait_recv()
            ring_step(1, xx, d, 0, None)
            to_partner(got)
        for s in range(1, 5):
            zr, zl = rem(z + NZ - s, NZ), rem(z + s, NZ)
            for i in (0, 1, 3, 2):
                xx = rem(x + NX - i, NX)
                ring_step(1, xx, i, s, None)
                to_partner(piece(1, xx, zr))
                if s < 4:
                    to_partner(piece(1, xx, zl))
        for i in range(4):
            ring_sent(1, rem(x + NX - i, NX), i)
        for d in (1, 3, 2):
            send(ref, ref, sX.at[d - 1, 0], rX.at[d - 1, 0], blk=x_peer(d)).wait_send()

    whole, theirs = X.at[pl.ds(core * HALF, HALF)], X.at[pl.ds((1 - core) * HALF, HALF)]
    swap.wait_send()
    send(theirs, theirs, sP, rP, blk=partner).wait_recv()
    send(whole, whole, sP, rP, blk=partner).wait_send()


def to_feat(S, f, sent, got):
    copies = []
    for d in (1, 2, 3):
        copies.append(send(S.at[f], S.at[f], sent.at[d - 1], got.at[d - 1], feat=rem(f + d, NF)))
        copies[-1].start()
    return copies


def from_feat(S, f, sent, got):
    for d in (1, 2, 3):
        ref = S.at[rem(f + NF - d, NF)]
        send(ref, ref, sent.at[d - 1], got.at[d - 1], feat=rem(f + d, NF)).wait_recv()


def scatter_blocks(G, H, XR, RR, RL, Fs, Fr, out, me, hooks, sH, rH, sX, rX, sR, rR, sL, rL, sy, ry):
    x, z, y, core, at = me
    right, left = at(x, rem(z + 1, NZ), y, core), at(x, rem(z + NZ - 1, NZ), y, core)
    partner = at(x, z, y, 1 - core)
    zs = [rem(z + o + NZ, NZ) for o in STEPS]
    mine, theirs = core * HALF, (1 - core) * HALF

    def given(j):
        return send(
            G.at[pl.ds(theirs + zs[j] * GROUP, GROUP)], H.at[pl.ds(zs[j] * GROUP, GROUP)],
            sH.at[j], rH.at[j], blk=partner,
        )

    def taken(j):
        ref = H.at[pl.ds(zs[j] * GROUP, GROUP)]
        send(ref, ref, sH.at[j], rH.at[j], blk=partner).wait_recv()
        def body(n, _):
            g = zs[j] * GROUP + n
            G[mine + g] = (G[mine + g].astype(F32) + H[g].astype(F32)).astype(BF16)
            return 0
        lax.fori_loop(0, GROUP, body, 0)

    for j in range(8):
        given(j).start()

    def x_peer(d):
        return at(rem(x + d, NX), z, y, core)

    def ring_copy(xx, i, j, way):
        base = mine + zs[j] * GROUP + xx * NY
        R, to, ss, rr, yy = (RR, right, sR, rR, 0) if way == 0 else (RL, left, sL, rL, 1)
        step = (j + 1) // 2
        if j == 0:
            return send(G.at[pl.ds(base + yy, 1)], R.at[0, i, pl.ds(yy, 1)], ss.at[i, 0], rr.at[i, 0], blk=to)
        return send(G.at[pl.ds(base, NY)], R.at[step, i], ss.at[i, step], rr.at[i, step], blk=to)

    def ring_wait(i, step, way):
        R, to, ss, rr, yy = (RR, right, sR, rR, 0) if way == 0 else (RL, left, sL, rL, 1)
        ref = R.at[0, i, pl.ds(yy, 1)] if step == 0 else R.at[step, i]
        send(ref, ref, ss.at[i, step], rr.at[i, step], blk=to).wait_recv()

    def ring(xx, i, j):
        base = mine + zs[j] * GROUP + xx * NY
        if j == 0:
            ring_copy(xx, i, 0, 0).start()
            ring_copy(xx, i, 0, 1).start()
        elif j < 7:
            way, step = (0, (j - 1) // 2) if j % 2 else (1, (j - 2) // 2)
            R = RR if way == 0 else RL
            ring_wait(i, step, way)
            if step == 0:
                G[base + way] = (G[base + way].astype(F32) + R[0, i, way].astype(F32)).astype(BF16)
            else:
                for n in range(NY):
                    G[base + n] = (G[base + n].astype(F32) + R[step, i, n].astype(F32)).astype(BF16)
            ring_copy(xx, i, j, way).start()
        else:
            ring_wait(i, 3, 0)
            ring_wait(i, 3, 1)

    def ring_total(xx, i, n):
        base = mine + zs[7] * GROUP + xx * NY
        return G[base + n].astype(F32) + RR[3, i, n].astype(F32) + RL[3, i, n].astype(F32)

    def ring_sent(xx, i):
        ring_copy(xx, i, 0, 0).wait_send()
        ring_copy(xx, i, 0, 1).wait_send()
        for j in range(1, 7):
            ring_copy(xx, i, j, 0 if j % 2 else 1).wait_send()

    def x_copy(d, j):
        src = G.at[pl.ds(mine + zs[j] * GROUP + rem(x + d, NX) * NY, NY)]
        return send(src, XR.at[d - 1, j], sX.at[d - 1, j], rX.at[d - 1, j], blk=x_peer(d))

    def x_wait(j):
        for d in (1, 3, 2):
            ref = XR.at[d - 1, j]
            send(ref, ref, sX.at[d - 1, j], rX.at[d - 1, j], blk=x_peer(d)).wait_recv()

    def x_total(start, j, n):
        return start + XR[0, j, n].astype(F32) + XR[1, j, n].astype(F32) + XR[2, j, n].astype(F32)

    @pl.when(core == 0)
    def _():
        def along_z(j):
            x_wait(j)
            base = mine + zs[j] * GROUP + x * NY
            for n in range(NY):
                G[base + n] = x_total(G[base + n].astype(F32), j, n).astype(BF16)
            ring(x, 0, j)

        for j in range(8):
            taken(j)
            for d in (1, 3, 2):
                x_copy(d, j).start()
            if j >= 2:
                along_z(j - 2)
        along_z(6)
        along_z(7)
        for n in range(NY):
            Fs[n] = ring_total(x, 0, n).astype(BF16)
        ring_sent(x, 0)
        for j in range(8):
            for d in (1, 3, 2):
                x_copy(d, j).wait_send()

    @pl.when(core == 1)
    def _():
        for j in range(8):
            taken(j)
            for i in range(4):
                ring(rem(x + i, NX), i, j)
                if j == 7:
                    for n in range(NY):
                        base = mine + zs[7] * GROUP + rem(x + i, NX) * NY
                        G[base + n] = ring_total(rem(x + i, NX), i, n).astype(BF16)
                    if i > 0:
                        x_copy(i, 7).start()
        x_wait(7)
        base = mine + zs[7] * GROUP + x * NY
        for n in range(NY):
            Fs[n] = x_total(G[base + n].astype(F32), 7, n).astype(BF16)
        for i in range(4):
            ring_sent(rem(x + i, NX), i)
        for d in (1, 3, 2):
            x_copy(d, 7).wait_send()

    last = send(Fs.at[1 - y], Fr, sy, ry, blk=at(x, z, 1 - y, core))
    last.start()
    last.wait()
    total = Fs[y].astype(F32) + Fr[...].astype(F32)
    out[:, 0:TILE] = total[0].astype(BF16)
    out[:, TILE:] = total[1].astype(BF16)
    for j in range(8):
        given(j).wait_send()


def kernel(
    feat_ref, near_hbm, far_hbm, place_ref, own_ref, table_ref, weight_ref, bias_ref, gout_ref,
    act_ref, gfeat_ref, gw_ref, gb_ref,
    near, far, X, G, H, XR, RR, RL, Fs, Fr, A, GP, WR, ga, parts, band,
    W0, W1, W2, W3, W5, W7, W8,
    local, sy, ry, sR, rR, sL, rL, sX, rX, sP, rP,
    sf, rf, sH, rH, tX, uX, tR, uR, tL, uL, sw, rw, sz, rz, sq, rq, sz2, rz2,
):
    b, f = lax.axis_index("blk"), lax.axis_index("feat")
    core, y, z, x = b % 2, (b // 2) % 2, (b // 4) % 8, b // 32

    def at(xx, zz, yy, cc):
        return ((xx * NZ + zz) * NY + yy) * NC + cc

    me = (x, z, y, core, at)
    partner = at(x, z, y, 1 - core)

    def slab(e):
        return rem(x + e // 2, NX), (y + e % 2) % 2

    load_far = pltpu.make_async_copy(far_hbm, far, local.at[0])
    load_near = pltpu.make_async_copy(near_hbm, near, local.at[1])
    load_far.start()
    load_near.start()

    barrier = pltpu.get_barrier_semaphore()
    for d in range(1, NZ):
        pl.semaphore_signal(barrier, 1, device_id={"blk": at(x, rem(z + d, NZ), y, core)}, device_id_type=pl.DeviceIdType.MESH)
    for e in range(1, 8):
        xx, yy = slab(e)
        pl.semaphore_signal(barrier, 1, device_id={"blk": at(xx, z, yy, core)}, device_id_type=pl.DeviceIdType.MESH)
    pl.semaphore_signal(barrier, 1, device_id={"blk": partner}, device_id_type=pl.DeviceIdType.MESH)
    for d in (1, 2, 3):
        pl.semaphore_signal(barrier, 1, device_id={"feat": rem(f + d, NF)}, device_id_type=pl.DeviceIdType.MESH)
    pl.semaphore_wait(barrier, 18)

    rows = []
    for d in (1, 2, 3):
        to = rem(f + d, NF)
        rows.append(send(weight_ref.at[pl.ds(pl.multiple_of(to * HD, HD), HD)], WR.at[f], sf.at[0, d - 1], rf.at[0, d - 1], feat=to))
        rows[-1].start()
    WR[f] = weight_ref[pl.ds(pl.multiple_of(f * HD, HD), HD), :]

    own = jnp.stack([feat_ref[:, 0:TILE], feat_ref[:, TILE:]])
    gather_blocks(own, X, me, sy.at[0], ry.at[0], sR, rR, sL, rL, sX, rX, sP, rP)

    load_near.wait()
    load_far.wait()
    total = jnp.zeros((HD, ROWS), F32)
    for s in range(BAND):
        c = rem(b + NB + s - 3, NB)
        spot = (c % 2) * HALF + ((c // 4) % 8) * GROUP + (c // 32) * NY + (c // 2) % 2
        total += dot(jnp.concatenate([X[spot, 0], X[spot, 1]], axis=1), near[s], NT)

    def far_forward(n, sums):
        low, high = sums
        for r in range(8):
            q = n * 8 + r
            p = place_ref[q]
            value = dot(X[p // 2, p % 2], far[q], NT)
            first = own_ref[q] == 0
            low += jnp.where(first, value, 0.0)
            high += jnp.where(first, 0.0, value)
        return low, high

    zero = jnp.zeros((HD, TILE), F32)
    low, high = lax.fori_loop(0, FAR // 8, far_forward, (zero, zero))
    A[f] = (total + jnp.concatenate([low, high], axis=1)).astype(BF16)
    first = to_feat(A, f, sf.at[1], rf.at[1])
    from_feat(A, f, sf.at[1], rf.at[1])

    gathered = A[...].reshape(NF * HD, ROWS)
    pre = dot(weight_ref[...], gathered, TN) + bias_ref[...]
    sig = jax.nn.sigmoid(pre)
    grad_pre = (gout_ref[...].astype(F32) * sig * (1.0 + pre * (1.0 - sig))).astype(BF16)
    GP[f] = grad_pre
    second = to_feat(GP, f, sf.at[2], rf.at[2])
    act_ref[...] = (pre * sig).astype(BF16)
    part = dot(gathered, grad_pre, NT)
    ones = dot(jnp.ones((8, ROWS), BF16), grad_pre, NT)
    W0[:, :, 0:8, 0:HD] = part[0:128].reshape(2, 8, 8, HD)
    W0[:, :, 0:8, HD:] = part[128:256].reshape(2, 8, 8, HD)
    side = jnp.concatenate([ones, ones], axis=1)
    for k in range(2):
        for n in range(8):
            W0[k, n, 8:16, :] = side
    halves = send(W0.at[1 - core], W1, sw.at[0], rw.at[0], blk=partner)
    halves.start()
    for d in (1, 2, 3):
        ref = WR.at[rem(f + NF - d, NF)]
        send(ref, ref, sf.at[0, d - 1], rf.at[0, d - 1], feat=rem(f + d, NF)).wait_recv()
    from_feat(GP, f, sf.at[2], rf.at[2])
    grad = jnp.zeros((HD, ROWS), F32)
    for n in range(NF):
        grad += dot(WR[n], GP[n], NN)
    grad = grad.astype(BF16)
    ga[0] = grad[:, 0:TILE]
    ga[1] = grad[:, TILE:]

    def far_backward(n, _):
        for r in range(8):
            q = n * 8 + r
            parts[q] = dot(ga[own_ref[q]], far[q], NN).astype(BF16)
        return 0

    lax.fori_loop(0, FAR // 8, far_backward, 0)
    parts[FAR] = jnp.zeros((HD, TILE), BF16)
    for s in range(BAND):
        value = dot(grad, near[s], NN)
        band[s, 0] = value[:, 0:TILE]
        band[s, 1] = value[:, TILE:]

    halves.wait()
    W2[...] = W0[core] + W1[...]
    to_z = []
    for d in range(1, NZ):
        zz = rem(z + d, NZ)
        to_z.append(send(W2.at[zz], W3.at[d - 1], sz.at[d - 1], rz.at[d - 1], blk=at(x, zz, y, core)))
        to_z[-1].start()

    def place(n, _):
        for r in range(4):
            c = n * 4 + r
            one, two = table_ref[0, c], table_ref[1, c]
            va, vb = parts[one // 2].astype(F32), parts[two // 2].astype(F32)
            ua, ub = one % 2 == 0, two % 2 == 0
            G[c, 0] = (jnp.where(ua, va, 0.0) + jnp.where(ub, vb, 0.0)).astype(BF16)
            G[c, 1] = (jnp.where(ua, 0.0, va) + jnp.where(ub, 0.0, vb)).astype(BF16)
        return 0

    lax.fori_loop(0, NB // 4, place, 0)
    for s in range(BAND):
        c = rem(b + NB + s - 3, NB)
        spot = (c % 2) * HALF + ((c // 4) % 8) * GROUP + (c // 32) * NY + (c // 2) % 2
        G[spot] = (G[spot].astype(F32) + band[s]).astype(BF16)

    for copy in to_z:
        copy.wait()
    mine = W2[z]
    for d in range(NZ - 1):
        mine += W3[d]
    W5[x * NY + y] = mine
    to_slab = []
    for e in range(1, 8):
        xx, yy = slab(e)
        to_slab.append(send(W5.at[x * NY + y], W5.at[x * NY + y], sq.at[e - 1], rq.at[e - 1], blk=at(xx, z, yy, core)))
        to_slab[-1].start()

    scatter_blocks(G, H, XR, RR, RL, Fs, Fr, gfeat_ref, me, None, sH, rH, tX, uX, tR, uR, tL, uL, sy.at[1], ry.at[1])

    for e in range(1, 8):
        xx, yy = rem(x + NX - e // 2, NX), (y + e % 2) % 2
        ref = W5.at[xx * NY + yy]
        send(ref, ref, sq.at[e - 1], rq.at[e - 1], blk=partner).wait_recv()
    total = W5[0]
    for n in range(1, 8):
        total += W5[n]
    W7[z] = total
    again = []
    for d in range(1, NZ):
        again.append(send(W7.at[z], W7.at[z], sz2.at[d - 1], rz2.at[d - 1], blk=at(x, rem(z + d, NZ), y, core)))
        again[-1].start()
    for d in range(1, NZ):
        ref = W7.at[rem(z + NZ - d, NZ)]
        send(ref, ref, sz2.at[d - 1], rz2.at[d - 1], blk=partner).wait_recv()
    final = send(W7, W8, sw.at[1], rw.at[1], blk=partner)
    final.start()
    final.wait_recv()
    for k in range(2):
        here = (k == core)
        value = jnp.where(here, W7[...], W8[...])
        rows_of = value[:, 0:8, :].reshape(64, 2 * HD)
        gw_ref[k * 64:k * 64 + 64, :] = rows_of[:, 0:HD]
        gw_ref[128 + k * 64:128 + k * 64 + 64, :] = rows_of[:, HD:]
    both = jnp.where(core == 0, W7[0, 8:16, :], W8[0, 8:16, :])
    gb_ref[...] = both[:, 0:HD]

    for copy in rows + first + second + to_slab + again:
        copy.wait_send()
    final.wait_send()


def on_device(features, near_tiles, far_tiles, far_source, far_index, weight, bias, grad_out):
    near = jnp.transpose(near_tiles, (1, 0, 2))
    c = far_source[:, 0]
    spot = (c % 2) * HALF + ((c // 4) % 8) * GROUP + (c // 32) * NY + (c // 2) % 2
    place = spot * 2 + far_index[:, 1]
    key = jnp.arange(FAR, dtype=jnp.int32) * 2 + far_index[:, 1]
    match = spot[None, :] == jnp.arange(NB, dtype=jnp.int32)[:, None]
    one = jnp.min(jnp.where(match, key[None, :], 2 * FAR), axis=1)
    two = jnp.max(jnp.where(match, key[None, :], -1), axis=1)
    two = jnp.where((two == one) | (two < 0), 2 * FAR, two)
    table = jnp.stack([one, two])
    vmem, smem, any_ = (pl.BlockSpec(memory_space=s) for s in (pltpu.VMEM, pltpu.SMEM, pl.ANY))
    dma = lambda *shape: pltpu.SemaphoreType.DMA(shape)
    block = (2, HD, TILE)
    act, gfeat, gw, gb = pl.pallas_call(
        kernel,
        out_shape=(
            jax.ShapeDtypeStruct((HD, ROWS), BF16),
            jax.ShapeDtypeStruct((HD, ROWS), BF16),
            jax.ShapeDtypeStruct((NF * HD, HD), F32),
            jax.ShapeDtypeStruct((8, HD), F32),
        ),
        in_specs=[vmem, any_, any_, smem, smem, smem, vmem, vmem, vmem],
        out_specs=(vmem,) * 4,
        scratch_shapes=[
            pltpu.VMEM((BAND, ROWS, ROWS), BF16),
            pltpu.VMEM((FAR, TILE, TILE), BF16),
            pltpu.VMEM((NB,) + block, BF16),
            pltpu.VMEM((NB,) + block, BF16),
            pltpu.VMEM((HALF,) + block, BF16),
            pltpu.VMEM((3, 8, NY) + block, BF16),
            pltpu.VMEM((4, NX, NY) + block, BF16),
            pltpu.VMEM((4, NX, NY) + block, BF16),
            pltpu.VMEM((NY,) + block, BF16),
            pltpu.VMEM(block, BF16),
            pltpu.VMEM((NF, HD, ROWS), BF16),
            pltpu.VMEM((NF, HD, ROWS), BF16),
            pltpu.VMEM((NF, HD, HD), BF16),
            pltpu.VMEM(block, BF16),
            pltpu.VMEM((FAR + 1, HD, TILE), BF16),
            pltpu.VMEM((BAND,) + block, F32),
            pltpu.VMEM((2, 8, 16, 128), F32),
            pltpu.VMEM((8, 16, 128), F32),
            pltpu.VMEM((8, 16, 128), F32),
            pltpu.VMEM((7, 16, 128), F32),
            pltpu.VMEM((8, 16, 128), F32),
            pltpu.VMEM((8, 16, 128), F32),
            pltpu.VMEM((8, 16, 128), F32),
            dma(2), dma(2), dma(2),
            dma(4, 4), dma(4, 4), dma(4, 4), dma(4, 4), dma(3, 8), dma(3, 8), pltpu.SemaphoreType.DMA, pltpu.SemaphoreType.DMA,
            dma(3, 3), dma(3, 3), dma(8), dma(8), dma(3, 8), dma(3, 8),
            dma(4, 4), dma(4, 4), dma(4, 4), dma(4, 4), dma(2), dma(2), dma(7), dma(7), dma(7), dma(7), dma(7), dma(7),
        ],
        compiler_params=pltpu.CompilerParams(
            collective_id=0, has_side_effects=True, vmem_limit_bytes=40 * 2**20
        ),
    )(features, near, far_tiles, place, far_index[:, 0], table, weight, bias[:, None], grad_out)
    return act, gfeat, gw, gb[0]


def solution(mesh):
    return jax.shard_map(
        on_device,
        mesh=mesh,
        in_specs=(
            P("feat", "blk"),
            P("blk", None, None),
            P("blk", None, None),
            P("blk", None),
            P("blk", None),
            P(None, "feat"),
            P("feat"),
            P("feat", "blk"),
        ),
        out_specs=(P("feat", "blk"), P("feat", "blk"), P(None, "feat"), P("feat")),
        check_vma=False,
    )
```

time: 1720 us -> 113 us (0.07)
  waiting for transfers between devices: 1000 us -> 0 us
  blocking collectives: 492 us -> 0 us
  starting transfers between devices: 109 us -> 0 us
  Pallas kernels: 0 us -> 102 us
  local copies, waits for them, and re-layouts: 57.3 us -> 9.33 us
  other arithmetic: 19.9 us -> 0.82 us
  matrix products: 17.6 us -> 0 us
    psum x1 -> x0, waiting for transfers between devices: 894 us -> none  [on_device(): grad_weight, grad_bias = lax.psum((weight_part, bias_part), 'blk')]
    psum x1 -> x0, blocking collectives: 479 us -> none  [on_device(): grad_weight, grad_bias = lax.psum((weight_part, bias_part), 'blk')]
    pallas_call x0 -> x1, Pallas kernels: none -> 102 us  [on_device(): pl.pallas_call(kernel, out_shape=(jax.ShapeDtypeStruct((HD, ROWS), BF16),...]
    ppermute x12 -> x0, waiting for transfers between devices: 72.4 us -> none  [shifted(): return lax.ppermute(block, axis, route)]
    ppermute x12 -> x0, starting transfers between devices: 64.8 us -> none  [shifted(): return lax.ppermute(block, axis, route)]
    all_to_all x3 -> x0, starting transfers between devices: 44.4 us -> none  [the longest x1 20.9 us: on_device(): lax.all_to_all(requests, 'blk', split_axis=0, concat_axis=0, tiled=True)]
    reduce_scatter x1 -> x0, waiting for transfers between devices: 24.3 us -> none  [on_device(): lax.psum_scatter(jnp.dot(weight, grad_pre, preferred_element_type=jnp.flo...]
    dot_general x8 -> x0, matrix products: 17.6 us -> none  [the longest x1 5.28 us: on_device(): jnp.einsum('khb,kab->kha', far_inputs, far_tiles, preferred_element_type=...]
  transfers between devices with their start and end apart: 17 -> 0, of which waited for: 4 -> 0; matrix products, arithmetic and copies ran while one was open for 1% -> 0% of each run, Pallas kernels for 0% -> 0%
where the time goes in v1:
time: 113 us
  Pallas kernels  102 us (90%)
  local copies, waits for them, and re-layouts  9.33 us (8%)
    pallas_call x1, Pallas kernels, on_device(): pl.pallas_call(kernel, out_shape=(jax.ShapeDtypeStruct((HD, ROWS), BF16),...  102 us
    unnamed x12, local copies, waits for them, and re-layouts  7.39 us

profile of v1, /device:TPU:1, one launch (start us, length us, event | category | flops | bytes accessed | tf_op | source)
XLA Modules:
  0.0 112.8 jit_solution(597948555377856255)
XLA Ops:
  0.6 0.7 slice_bitcast_fusion.1.own_ref
  1.3 0.7 bitcast_add_fusion.1
  2.0 0.1 select_reduce_fusion.1
  2.1 0.7 copy.16.bias_ref
  2.9 0.9 copy.15.weight_ref
  3.8 0.0 copy-start
  3.8 1.9 %copy-done = bf16[96,128,128]{2,1,0:T(8,128)(2,1)S(1)} copy-done((bf16[96,128,128]{2,1,0:T(8,128)(2,1)S(1)}, bf16[96,128,128]{2,1,0:T(8,128)(2,1)}, u32[]{:S(2)}) %copy-start) | copy-done | bytes 3145752
  5.7 0.0 copy-start.1
  5.7 1.2 %copy-done.1 = bf16[256,7,256]{2,0,1:T(8,128)(2,1)S(1)} copy-done((bf16[256,7,256]{2,0,1:T(8,128)(2,1)S(1)}, bf16[256,7,256]{2,0,1:T(8,128)(2,1)}, u32[]{:S(2)}) %copy-start.1) | copy-done | bytes 917528
  6.8 0.0 copy-start.2
  6.8 0.8 copy-done.2
  7.6 0.0 copy-start.3
  7.6 0.8 copy-done.3
  8.4 102.0 %shard_map.111 = (bf16[64,256]{1,0:T(8,128)(2,1)S(1)}, bf16[64,256]{1,0:T(8,128)(2,1)S(1)}, f32[256,64]{1,0:T(8,128)S(1)}, f32[8,64]{1,0:T(8,128)S(1)}) custom-call(bf16[64,256]{1,0:T(8,128)(2,1)S(1)} %copy-done.2, bf16[7,256,256]{2,1,0:T(8,128)(2,1)S(1)} %bitcast.34, bf16[96,128,128]{2,1,0:T(8,128)(2,1)S(1)} %copy-done, s32[96]{0:T(128)S(1)} %get-tuple-element.22.place_ref, ...), custom_call_target="tpu_custom_call" | custom-call | tf_op jit(solution)/shard_map/pallas_call | solution.py:493
  110.4 0.5 slice_bitcast_fusion
  110.9 0.7 copy.17
  111.6 0.6 copy.20
  112.2 0.6 copy.21
  (2 shorter events, 0.0 us)
Async XLA Ops:
  3.8 1.9 %copy-start = (bf16[96,128,128]{2,1,0:T(8,128)(2,1)S(1)}, bf16[96,128,128]{2,1,0:T(8,128)(2,1)}, u32[]{:S(2)}) copy-start(bf16[96,128,128]{2,1,0:T(8,128)(2,1)} %far_hbm.1) | copy-start | bytes 9437188
  5.7 1.2 %copy-start.1 = (bf16[256,7,256]{2,0,1:T(8,128)(2,1)S(1)}, bf16[256,7,256]{2,0,1:T(8,128)(2,1)}, u32[]{:S(2)}) copy-start(bf16[256,7,256]{2,0,1:T(8,128)(2,1)} %param.9) | copy-start | bytes 2752516
  6.8 0.8 copy-start.2
  7.6 0.8 copy-start.3

commit v2 on v0

v2 whole, which is shorter than its diff:
```python
import functools

import jax
import jax.numpy as jnp
from jax import lax
from jax.experimental import pallas as pl
from jax.experimental.pallas import tpu as pltpu
from jax.sharding import PartitionSpec as P

NX, NZ, NY, NC = 4, 8, 2, 2
NB = NX * NZ * NY * NC
HALF = NB // NC
GROUP = NX * NY
FAR = 96
BAND = 7
NF = 4
HD = 64
TILE = 128
ROWS = 256
F32 = jnp.float32
BF16 = jnp.bfloat16
NN = (((1,), (0,)), ((), ()))
NT = (((1,), (1,)), ((), ()))
TN = (((0,), (0,)), ((), ()))
STEPS = (4, 3, -3, 2, -2, 1, -1, 0)


def dot(a, b, dims):
    return lax.dot_general(a, b, dims, preferred_element_type=F32)


def send(src, dst, sent, got, **where):
    return pltpu.make_async_remote_copy(
        src_ref=src, dst_ref=dst, send_sem=sent, recv_sem=got,
        device_id=where, device_id_type=pl.DeviceIdType.MESH,
    )


def rem(a, n):
    return lax.rem(a, jnp.int32(n))


def within(n, most):
    return jnp.minimum(jnp.maximum(n, 0), most)


def spot_of(c):
    return (c % 2) * HALF + ((c // 4) % 8) * GROUP + ((c // 2) % 2) * NX + c // 32


def gather_blocks(X, me, sy, ry, sR, rR, sL, rL, sXR, rXR, sXL, rXL, sP, rP):
    x, z, y, core, at = me
    east, west = at(rem(x + 1, NX), z, y, core), at(rem(x + NX - 1, NX), z, y, core)
    partner, across = at(x, z, y, 1 - core), at(x, z, 1 - y, core)
    ys = (y, 1 - y)

    def block(k, xx, zz, w):
        return k * HALF + zz * GROUP + ys[w] * NX + xx

    def whole(k, xx, zz, w):
        return X.at[block(k, xx, zz, w)]

    swap = send(whole(core, x, z, 0), whole(core, x, z, 0), sy, ry, blk=across)
    swap.start()

    def swapped():
        send(whole(core, x, z, 1), whole(core, x, z, 1), sy, ry, blk=across).wait_recv()

    def hand(k, zz, w, wait=False):
        ref = X.at[pl.ds(k * HALF + zz * GROUP + ys[w] * NX, NX)]
        copy = send(ref, ref, sP, rP, blk=partner)
        copy.start()

    def ring_parts(k, xx, i, w, wide):
        out = []
        for sign, ss, rr in ((1, sR, rR), (-1, sL, rL)):
            def step(n, zd, hops, half, ss=ss, rr=rr, sign=sign):
                src = whole(k, xx, rem(z + NZ - sign * zd, NZ), w)
                src = src if half is None else src.at[half]
                return send(src, src, ss.at[w, i, n], rr.at[w, i, n], blk=at(x, rem(z + NZ + sign * hops, NZ), y, core))

            half = 0 if sign == 1 else 1
            out.append((
                functools.partial(step, 0, 0, 1, None),
                functools.partial(step, 1, 0, 2, None) if wide else functools.partial(step, 1, 1, 1, None),
                functools.partial(step, 2, 2, 1, None),
                functools.partial(step, 3, 2, 2, half),
            ))
        return out

    def ring_got(k, xx, i, w, n):
        for sign, ss, rr, u in ((1, sR, rR, 0), (-1, sL, rL, 1)):
            ref = whole(k, xx, rem(z + NZ - sign * (n + 1), NZ), w)
            ref = ref if n < 3 else ref.at[u]
            send(ref, ref, ss.at[w, i, n], rr.at[w, i, n], blk=partner).wait_recv()

    def ring_start(k, xx, i, w, wide):
        parts = ring_parts(k, xx, i, w, wide)
        if wide:
            parts[0][1]().start()
            parts[1][1]().start()
        parts[0][0]().start()
        parts[1][0]().start()

    def ring_second(k, xx, i, w):
        ring_got(k, xx, i, w, 0)
        for part in ring_parts(k, xx, i, w, False):
            part[1]().start()

    def ring_third(k, xx, i, w):
        ring_got(k, xx, i, w, 1)
        for part in ring_parts(k, xx, i, w, True):
            part[3]().start()
            part[2]().start()

    def ring_sent(k, xx, i, w, wide):
        for part in ring_parts(k, xx, i, w, wide):
            for copy in part:
                copy().wait_send()

    def x_step(k, zz, j, w, s, what):
        for xx, ss, rr, to, u in ((rem(x + NX - s, NX), sXR, rXR, east, 0), (rem(x + s, NX), sXL, rXL, west, 1)):
            ref = whole(k, xx, zz, w)
            if what == "go" and s > 0:
                got = ref if s < 2 else ref.at[u]
                send(got, got, ss.at[w, j, s - 1], rr.at[w, j, s - 1], blk=to).wait_recv()
            if s < 2:
                out = ref if s < 1 else ref.at[u]
                copy = send(out, out, ss.at[w, j, s], rr.at[w, j, s], blk=to)
                copy.start() if what == "go" else copy.wait_send()

    def places(s):
        if s == 0:
            return [(z, 0)]
        if s == 4:
            return [(rem(z + 4, NZ), 7)]
        return [(rem(z + NZ - s, NZ), 2 * s - 1), (rem(z + s, NZ), 2 * s)]

    def across_x(w):
        ref = whole(1, x, z, w)
        return (
            send(ref, ref, sXR.at[w, 0, 0], rXR.at[w, 0, 0], blk=east),
            send(ref, ref, sXL.at[w, 0, 0], rXL.at[w, 0, 0], blk=west),
            send(ref, ref, sXR.at[w, 0, 1], rXR.at[w, 0, 1], blk=at(rem(x + 2, NX), z, y, core)),
        )

    def from_x(w, i):
        ref = whole(1, rem(x + NX - i, NX), z, w)
        ss, rr, n = ((sXR, rXR, 0), (sXR, rXR, 1), (sXL, rXL, 0))[i - 1]
        send(ref, ref, ss.at[w, 0, n], rr.at[w, 0, n], blk=partner).wait_recv()

    def hop(s, w, n):
        for zz, j in places(s):
            x_step(0, zz, j, w, n, "go")
            if n == 2:
                hand(0, zz, w)

    @pl.when(core == 0)
    def _():
        def got(n, w):
            ring_got(0, x, 0, w, n)
            hop(n + 1, w, 0)

        def third(w):
            ring_third(0, x, 0, w)
            hop(2, w, 0)

        ring_start(0, x, 0, 0, True)
        hop(0, 0, 0)
        third(0)
        got(0, 0)
        swapped()
        ring_start(0, x, 0, 1, True)
        hop(0, 1, 0)
        hop(0, 0, 1)
        got(2, 0)
        got(3, 0)
        hop(2, 0, 1)
        hop(1, 0, 1)
        hop(0, 0, 2)
        third(1)
        got(0, 1)
        for s, w, n in ((0, 1, 1), (3, 0, 1), (4, 0, 1), (2, 0, 2), (1, 0, 2)):
            hop(s, w, n)
        got(2, 1)
        got(3, 1)
        for s, w, n in (
            (2, 1, 1), (1, 1, 1), (3, 0, 2), (4, 0, 2), (0, 1, 2), (3, 1, 1), (4, 1, 1),
            (2, 1, 2), (1, 1, 2), (3, 1, 2), (4, 1, 2),
        ):
            hop(s, w, n)

    @pl.when(core == 1)
    def _():
        every = (0, 1, 3, 2)

        def xs(i):
            return rem(x + NX - i, NX)

        def spread(w):
            for i in (1, 3, 2):
                from_x(w, i)
                ring_start(1, xs(i), i, w, False)
            hand(1, z, w)

        def second(w, which):
            for i in which:
                ring_second(1, xs(i), i, w)

        def third(w, which):
            for i in which:
                ring_third(1, xs(i), i, w)

        def done(w, n):
            for i in every:
                ring_got(1, xs(i), i, w, n)
            for zz, j in places(n + 1):
                hand(1, zz, w)

        def along(w, n):
            for zz, j in places(n + 1):
                hand(1, zz, w)

        for copy in across_x(0):
            copy.start()
        ring_start(1, x, 0, 0, False)
        spread(0)
        second(0, (0,))
        swapped()
        for copy in across_x(1):
            copy.start()
        ring_start(1, x, 0, 1, False)
        second(0, (1, 3, 2))
        along(0, 0)
        third(0, (0,))
        spread(1)
        second(1, (0,))
        third(0, (1, 3, 2))
        along(0, 1)
        second(1, (1, 3, 2))
        along(1, 0)
        third(1, (0,))
        done(0, 2)
        done(0, 3)
        third(1, (1, 3, 2))
        along(1, 1)
        done(1, 2)
        done(1, 3)

    theirs = X.at[pl.ds((1 - core) * HALF, HALF)]
    send(theirs, theirs, sP, rP, blk=partner).wait_recv()

    def finish():
        swap.wait_send()
        ours = X.at[pl.ds(core * HALF, HALF)]
        send(ours, ours, sP, rP, blk=partner).wait_send()

        @pl.when(core == 0)
        def _():
            for w in (0, 1):
                ring_sent(0, x, 0, w, True)
                for s in range(5):
                    for zz, j in places(s):
                        x_step(0, zz, j, w, 0, "end")
                        x_step(0, zz, j, w, 1, "end")

        @pl.when(core == 1)
        def _():
            for w in (0, 1):
                for copy in across_x(w):
                    copy.wait_send()
                for i in range(4):
                    ring_sent(1, rem(x + NX - i, NX), i, w, False)

    return finish


def to_feat(S, f, sent, got):
    copies = []
    for d in (1, 2, 3):
        copies.append(send(S.at[f], S.at[f], sent.at[d - 1], got.at[d - 1], feat=rem(f + d, NF)))
        copies[-1].start()
    return copies


def from_feat(S, f, sent, got):
    for d in (1, 2, 3):
        ref = S.at[rem(f + NF - d, NF)]
        send(ref, ref, sent.at[d - 1], got.at[d - 1], feat=rem(f + d, NF)).wait_recv()


def add_to(G, at, u, *more):
    if u is None:
        total = G[at].astype(F32)
        for m in more:
            total += m.astype(F32)
        G[at] = total.astype(BF16)
    else:
        total = G[at, u].astype(F32)
        for m in more:
            total += m.astype(F32)
        G[at, u] = total.astype(BF16)


def scatter_blocks(G, H, XE, XW, RR, RL, Fs, Fr, out, me, hooks, sH, rH, sXR, rXR, sXL, rXL, sR, rR, sL, rL, sy, ry):
    x, z, y, core, at = me
    east, west = at(rem(x + 1, NX), z, y, core), at(rem(x + NX - 1, NX), z, y, core)
    partner, across = at(x, z, y, 1 - core), at(x, z, 1 - y, core)
    zs = [rem(z + o + NZ, NZ) for o in STEPS]
    ys = (1 - y, y)
    mine, theirs = core * HALF, (1 - core) * HALF

    def block(xx, j, w):
        return mine + zs[j] * GROUP + ys[w] * NX + xx

    def given(zz, yy, n):
        ref = G.at[pl.ds(theirs + zz * GROUP + yy * NX, NX)]
        return send(ref, H.at[pl.ds(zz * GROUP + yy * NX, NX)], sH.at[n], rH.at[n], blk=partner)

    def taken(j, w):
        base = zs[j] * GROUP + ys[w] * NX
        ref = H.at[pl.ds(base, NX)]
        send(ref, ref, sH.at[j * 2 + w], rH.at[j * 2 + w], blk=partner).wait_recv()
        for n in range(NX):
            add_to(G, mine + base + n, None, H[base + n])

    def ring_copy(xx, i, w, n, way, wide):
        R, ss, rr, sign = (RR, sR, rR, 1) if way == 0 else (RL, sL, rL, -1)
        src = G.at[mine + rem(z + NZ + sign * (n + 1), NZ) * GROUP + ys[w] * NX + xx]
        dst = R.at[w, n, i]
        if n == 3:
            src, dst = src.at[way], dst.at[way]
        hops = 2 if n == 3 or (n == 1 and wide) else 1
        return send(src, dst, ss.at[w, i, n], rr.at[w, i, n], blk=at(x, rem(z + NZ + sign * hops, NZ), y, core))

    def ring_wait(i, w, n, way):
        R, ss, rr = (RR, sR, rR) if way == 0 else (RL, sL, rL)
        ref = R.at[w, n, i, way] if n == 3 else R.at[w, n, i]
        send(ref, ref, ss.at[w, i, n], rr.at[w, i, n], blk=partner).wait_recv()

    def ring(xx, i, j, w, wide):
        if j == 0:
            for way in (0, 1):
                ring_copy(xx, i, w, 3, way, wide).start()
            return
        if j == 7:
            total = G[block(xx, 7, w)].astype(F32)
            for way, R in ((0, RR), (1, RL)):
                for n in (0, 1) if wide else (0,):
                    ring_wait(i, w, n, way)
                    total += R[w, n, i].astype(F32)
            return total
        way, n = (j + 1) % 2, 2 - (j - 1) // 2
        R, base = (RR, RL)[way], block(xx, j, w)
        if n == 1:
            ring_wait(i, w, 3, way)
            ring_wait(i, w, 2, way)
            add_to(G, base, way, R[w, 3, i, way])
            add_to(G, base, None, R[w, 2, i])
        if n == 0 and not wide:
            ring_wait(i, w, 1, way)
            add_to(G, base, None, R[w, 1, i])
        ring_copy(xx, i, w, n, way, wide).start()

    def ring_sent(xx, i, w, wide):
        for n in range(4):
            for way in (0, 1):
                ring_copy(xx, i, w, n, way, wide).wait_send()

    def x_copies(j, w, s):
        far, near_e, near_w = block(rem(x + 2, NX), j, w), block(rem(x + 1, NX), j, w), block(rem(x + NX - 1, NX), j, w)
        n = j * 2 + w
        if s == 0:
            return (send(G.at[far, 0], XE.at[n, 0, 0], sXR.at[n, 0], rXR.at[n, 0], blk=east),
                    send(G.at[far, 1], XW.at[n, 0, 1], sXL.at[n, 0], rXL.at[n, 0], blk=west))
        return (send(G.at[near_e], XE.at[n, 1], sXR.at[n, 1], rXR.at[n, 1], blk=east),
                send(G.at[near_w], XW.at[n, 1], sXL.at[n, 1], rXL.at[n, 1], blk=west))

    def x_step(j, w, s):
        n = j * 2 + w
        if s > 0:
            for copy in x_copies(j, w, s - 1):
                copy.wait_recv()
        if s == 1:
            add_to(G, block(rem(x + 1, NX), j, w), 0, XE[n, 0, 0])
            add_to(G, block(rem(x + NX - 1, NX), j, w), 1, XW[n, 0, 1])
        if s < 2:
            for copy in x_copies(j, w, s):
                copy.start()

    def x_total(j, w):
        n = j * 2 + w
        return G[block(x, j, w)].astype(F32) + XE[n, 1].astype(F32) + XW[n, 1].astype(F32)

    def across_x(w):
        n = 14 + w
        return (
            send(G.at[block(rem(x + 1, NX), 7, w)], XE.at[n, 1], sXR.at[n, 1], rXR.at[n, 1], blk=east),
            send(G.at[block(rem(x + NX - 1, NX), 7, w)], XW.at[n, 1], sXL.at[n, 1], rXL.at[n, 1], blk=west),
            send(G.at[block(rem(x + 2, NX), 7, w)], XE.at[n, 0], sXR.at[n, 0], rXR.at[n, 0], blk=at(rem(x + 2, NX), z, y, core)),
        )

    def from_x(w):
        for copy in across_x(w):
            copy.wait_recv()
        return x_total(7, w) + XE[14 + w, 0].astype(F32)

    order = tuple((j, w) for w in range(2) for j in range(8))
    last = send(Fs.at[0], Fr, sy, ry, blk=across)

    def deliver(w, total):
        Fs[w] = total.astype(BF16)
        if w == 0:
            last.start()

    def run():
        @pl.when(core == 0)
        def _():
            for n in range(len(order) + 8):
                if n < len(order):
                    taken(*order[n])
                    x_step(*order[n], 0)
                if 0 <= n - 4 < len(order):
                    x_step(*order[n - 4], 1)
                if 0 <= n - 8:
                    j, w = order[n - 8]
                    x_step(j, w, 2)
                    G[block(x, j, w)] = x_total(j, w).astype(BF16)
                    total = ring(x, 0, j, w, True)
                    if j == 7:
                        deliver(w, total)
                if n in hooks:
                    hooks[n]()

        @pl.when(core == 1)
        def _():
            for n, (j, w) in enumerate(order):
                taken(j, w)
                for i in (2, 1, 3, 0):
                    xx = rem(x + i, NX)
                    total = ring(xx, i, j, w, False)
                    if j == 7:
                        G[block(xx, 7, w)] = total.astype(BF16)
                if j == 7:
                    for copy in across_x(w):
                        copy.start()
                if (j, w) == (4, 1):
                    deliver(0, from_x(0))
                if (j, w) == (7, 1):
                    deliver(1, from_x(1))
                if n in hooks:
                    hooks[n]()

        last.wait_recv()
        total = Fs[1].astype(F32) + Fr[...].astype(F32)
        out[:, 0:TILE] = total[0].astype(BF16)
        out[:, TILE:] = total[1].astype(BF16)

    def finish():
        last.wait_send()
        for j in range(8):
            for w in range(2):
                given(zs[j], ys[w], j * 2 + w).wait_send()

        @pl.when(core == 0)
        def _():
            for w in range(2):
                ring_sent(x, 0, w, True)
                for j in range(8):
                    for s in range(2):
                        for copy in x_copies(j, w, s):
                            copy.wait_send()

        @pl.when(core == 1)
        def _():
            for w in range(2):
                for i in range(4):
                    ring_sent(rem(x + i, NX), i, w, False)
                for copy in across_x(w):
                    copy.wait_send()

    return given, run, finish


def kernel(
    feat_hbm, near_hbm, far_hbm, source_ref, index_ref, source_row, index_row, weight_hbm, bias_ref, gout_hbm,
    act_ref, gfeat_ref, gw_ref, gb_ref,
    near, far, feat_in, gout_in, X, G, H, XE, XW, RR, RL, Fs, Fr, A, GP, WR, WT, ga, parts, band, rows_v, table,
    W0, W1, W2, W3, W5, W7, W8,
    local, sy, ry, sR, rR, sL, rL, sXR, rXR, sXL, rXL, sP, rP,
    sf, rf, sH, rH, tXR, uXR, tXL, uXL, tR, uR, tL, uL, sw, rw, sz, rz, sq, rq, sz2, rz2,
):
    b, f = lax.axis_index("blk"), lax.axis_index("feat")
    core, y, z, x = b % 2, (b // 2) % 2, (b // 4) % 8, b // 32

    def at(xx, zz, yy, cc):
        return ((xx * NZ + zz) * NY + yy) * NC + cc

    me = (x, z, y, core, at)
    partner = at(x, z, y, 1 - core)

    def slab(e):
        return rem(x + e // 2, NX), (y + e % 2) % 2

    def signal(**where):
        pl.semaphore_signal(barrier, 1, device_id=where, device_id_type=pl.DeviceIdType.MESH)

    barrier = pltpu.get_barrier_semaphore()
    signal(blk=partner)
    for e in range(1, 8):
        xx, yy = slab(e)
        signal(blk=at(xx, z, yy, core))
    for d in range(1, NZ):
        signal(blk=at(x, rem(z + d, NZ), y, core))
    for d in (1, 2, 3):
        signal(feat=rem(f + d, NF))

    load_feat = pltpu.make_async_copy(feat_hbm, feat_in, local.at[0])
    load_weight = pltpu.make_async_copy(weight_hbm, WR.at[f], local.at[1])
    load_gout = pltpu.make_async_copy(gout_hbm, gout_in, local.at[2])
    load_near = pltpu.make_async_copy(near_hbm, near, local.at[3])
    load_far = pltpu.make_async_copy(far_hbm, far, local.at[4])
    for load in (load_feat, load_weight, load_gout, load_near, load_far):
        load.start()

    places = jnp.broadcast_to(spot_of(source_row[...]), (NB, FAR))
    keys = jnp.broadcast_to((lax.broadcasted_iota(jnp.int32, (1, FAR), 1) * 2 + index_row[1:2, :]).astype(F32), (NB, FAR))
    match = places == lax.broadcasted_iota(jnp.int32, (NB, FAR), 0)
    one = jnp.min(jnp.where(match, keys, 2.0 * FAR), axis=1, keepdims=True)
    two = jnp.max(jnp.where(match, keys, -1.0), axis=1, keepdims=True)
    two = jnp.where((two == one) | (two < 0.0), 2.0 * FAR, two)
    rows_v[0:8] = jnp.transpose(jnp.broadcast_to(one, (NB, NB)))[0:8].astype(jnp.int32)
    rows_v[8:16] = jnp.transpose(jnp.broadcast_to(two, (NB, NB)))[0:8].astype(jnp.int32)
    load_table = pltpu.make_async_copy(rows_v, table, local.at[5])
    load_table.start()
    bias = jnp.transpose(jnp.broadcast_to(jnp.concatenate([bias_ref[...], bias_ref[...]], axis=1), (2 * HD, 2 * HD)))[0:HD]
    bias = jnp.concatenate([bias, bias], axis=1)

    load_feat.wait()
    own = core * HALF + z * GROUP + y * NX + x
    X[own, 0] = feat_in[:, 0:TILE]
    X[own, 1] = feat_in[:, TILE:]
    pl.semaphore_wait(barrier, 18)

    gathered_all = gather_blocks(X, me, sy.at[0], ry.at[0], sR, rR, sL, rL, sXR, rXR, sXL, rXL, sP, rP)

    load_weight.wait()
    zero_th = to_feat(WR, f, sf.at[0], rf.at[0])
    load_near.wait()
    load_far.wait()
    total = jnp.zeros((HD, ROWS), F32)
    for s in range(BAND):
        spot = spot_of(rem(b + NB + s - 3, NB))
        total += dot(jnp.concatenate([X[spot, 0], X[spot, 1]], axis=1), near[s], NT)

    def far_forward(n, sums):
        low, high = sums
        for r in range(8):
            q = n * 8 + r
            value = dot(X[within(spot_of(source_ref[0, q]), NB - 1), within(index_ref[1, q], 1)], far[q], NT)
            first = index_ref[0, q] == 0
            low += jnp.where(first, value, 0.0)
            high += jnp.where(first, 0.0, value)
        return low, high

    zero = jnp.zeros((HD, TILE), F32)
    low, high = lax.fori_loop(0, FAR // 8, far_forward, (zero, zero))
    A[f] = (total + jnp.concatenate([low, high], axis=1)).astype(BF16)
    first = to_feat(A, f, sf.at[1], rf.at[1])
    from_feat(WR, f, sf.at[0], rf.at[0])
    WT[...] = jnp.transpose(WR[...].reshape(NF * HD, NF * HD).astype(F32))
    load_gout.wait()
    from_feat(A, f, sf.at[1], rf.at[1])

    gathered = A[...].reshape(NF * HD, ROWS)
    pre = dot(WR[f], gathered, NN) + bias
    sig = jax.nn.sigmoid(pre)
    grad_pre = (gout_in[...].astype(F32) * sig * (1.0 + pre * (1.0 - sig))).astype(BF16)
    GP[f] = grad_pre
    second = to_feat(GP, f, sf.at[2], rf.at[2])
    part = dot(grad_pre, gathered, NT)
    ones = dot(jnp.ones((8, ROWS), BF16), grad_pre, NT)
    side = jnp.concatenate([ones, ones], axis=1)
    for k in range(2):
        W0[k, :, 0:8, :] = part[:, k * 128:k * 128 + 128].reshape(8, 8, 128)
        for n in range(8):
            W0[k, n, 8:16, :] = side
    halves = send(W0.at[1 - core], W1, sw.at[0], rw.at[0], blk=partner)
    halves.start()
    act_ref[...] = (pre * sig).astype(BF16)
    from_feat(GP, f, sf.at[2], rf.at[2])
    own_rows = WT[pl.ds(pl.multiple_of(f * HD, HD), HD), :].astype(BF16)
    grad = dot(own_rows, GP[...].reshape(NF * HD, ROWS), NN).astype(BF16)
    ga[0] = grad[:, 0:TILE]
    ga[1] = grad[:, TILE:]

    halves.wait_recv()
    W2[...] = W0[core] + W1[...]
    to_z = []
    for d in range(1, NZ):
        zz = rem(z + d, NZ)
        to_z.append(send(W2.at[zz], W3.at[d - 1], sz.at[d - 1], rz.at[d - 1], blk=at(x, zz, y, core)))
        to_z[-1].start()

    def far_backward(n, _):
        for r in range(8):
            q = n * 8 + r
            parts[q] = dot(ga[within(index_ref[0, q], 1)], far[q], NN).astype(BF16)
        return 0

    lax.fori_loop(0, FAR // 8, far_backward, 0)
    parts[FAR] = jnp.zeros((HD, TILE), BF16)
    for s in range(BAND):
        value = dot(grad, near[s], NN)
        band[s, 0] = value[:, 0:TILE]
        band[s, 1] = value[:, TILE:]

    to_slab, again = [], []
    for e in range(1, 8):
        xx, yy = slab(e)
        to_slab.append(send(W5.at[x * NY + y], W5.at[x * NY + y], sq.at[e - 1], rq.at[e - 1], blk=at(xx, z, yy, core)))
    for d in range(1, NZ):
        again.append(send(W7.at[z], W7.at[z], sz2.at[d - 1], rz2.at[d - 1], blk=at(x, rem(z + d, NZ), y, core)))
    final = send(W7, W8, sw.at[1], rw.at[1], blk=partner)

    def sum_z():
        for copy in to_z:
            copy.wait_recv()
        mine = W2[z]
        for d in range(NZ - 1):
            mine += W3[d]
        W5[x * NY + y] = mine
        for copy in to_slab:
            copy.start()

    def sum_slab():
        for e in range(1, 8):
            ref = W5.at[rem(x + NX - e // 2, NX) * NY + (y + e % 2) % 2]
            send(ref, ref, sq.at[e - 1], rq.at[e - 1], blk=partner).wait_recv()
        total = W5[0]
        for n in range(1, 8):
            total += W5[n]
        W7[z] = total
        for copy in again:
            copy.start()

    def spread_z():
        for d in range(1, NZ):
            ref = W7.at[rem(z + NZ - d, NZ)]
            send(ref, ref, sz2.at[d - 1], rz2.at[d - 1], blk=partner).wait_recv()
        final.start()

    sum_z()
    hooks = {6: sum_slab, 14: spread_z}
    given, run, sent = scatter_blocks(
        G, H, XE, XW, RR, RL, Fs, Fr, gfeat_ref, me, hooks,
        sH, rH, tXR, uXR, tXL, uXL, tR, uR, tL, uL, sy.at[1], ry.at[1],
    )

    def place(c):
        one, two = table[0, c], table[8, c]
        va, vb = parts[within(one // 2, FAR)].astype(F32), parts[within(two // 2, FAR)].astype(F32)
        ua, ub = one % 2 == 0, two % 2 == 0
        G[c, 0] = (jnp.where(ua, va, 0.0) + jnp.where(ub, vb, 0.0)).astype(BF16)
        G[c, 1] = (jnp.where(ua, 0.0, va) + jnp.where(ub, 0.0, vb)).astype(BF16)

    def group(j, w):
        return rem(z + 4 + j // 2 + (j % 2) * (NZ - j), NZ), (1 - y, y)[w]

    def fill(j, w):
        zz, yy = group(j, w)
        for k in (1 - core, core):
            for r in range(NX):
                place(k * HALF + zz * GROUP + yy * NX + r)

    def give(j, w):
        zz, yy = group(j, w)
        given(zz, yy, j * 2 + w).start()

    def fill_and_give(w, j, _):
        fill(j, w)
        give(j, w)
        return 0

    def fill_near(j, _):
        fill(j, 0)
        fill(j, 1)
        return 0

    load_table.wait()
    lax.fori_loop(0, 5, functools.partial(fill_and_give, 0), 0)
    lax.fori_loop(5, 8, fill_near, 0)
    for s in range(BAND):
        spot = spot_of(rem(b + NB + s - 3, NB))
        G[spot] = (G[spot].astype(F32) + band[s]).astype(BF16)
    for j in (5, 6, 7):
        give(j, 0)
    lax.fori_loop(0, 5, functools.partial(fill_and_give, 1), 0)
    for j in (5, 6, 7):
        give(j, 1)

    run()
    final.wait_recv()
    for k in range(2):
        value = jnp.where(core == k, W7[...], W8[...])
        gw_ref[:, k * 128:k * 128 + 128] = value[:, 0:8, :].reshape(HD, 128)
    gb_ref[...] = jnp.where(core == 0, W7[0, 8:9, :], W8[0, 8:9, :])[:, 0:HD]

    gathered_all()
    sent()
    halves.wait_send()
    for copy in zero_th + first + second + to_z + to_slab + again + [final]:
        copy.wait_send()


def on_device(features, near_tiles, far_tiles, far_source, far_index, weight, bias, grad_out):
    near = jnp.transpose(near_tiles, (1, 0, 2))
    source, index = far_source.T, far_index.T
    vmem, smem, any_ = (pl.BlockSpec(memory_space=s) for s in (pltpu.VMEM, pltpu.SMEM, pl.ANY))
    dma = lambda *shape: pltpu.SemaphoreType.DMA(shape)
    one = pltpu.SemaphoreType.DMA
    block = (2, HD, TILE)
    act, gfeat, gw, gb = pl.pallas_call(
        kernel,
        out_shape=(
            jax.ShapeDtypeStruct((HD, ROWS), BF16),
            jax.ShapeDtypeStruct((HD, ROWS), BF16),
            jax.ShapeDtypeStruct((HD, NF * HD), F32),
            jax.ShapeDtypeStruct((1, HD), F32),
        ),
        in_specs=[any_, any_, any_, smem, smem, vmem, vmem, any_, vmem, any_],
        out_specs=(vmem,) * 4,
        scratch_shapes=[
            pltpu.VMEM((BAND, ROWS, ROWS), BF16),
            pltpu.VMEM((FAR, TILE, TILE), BF16),
            pltpu.VMEM((HD, ROWS), BF16),
            pltpu.VMEM((HD, ROWS), BF16),
            pltpu.VMEM((NB,) + block, BF16),
            pltpu.VMEM((NB,) + block, BF16),
            pltpu.VMEM((HALF,) + block, BF16),
            pltpu.VMEM((16, 2) + block, BF16),
            pltpu.VMEM((16, 2) + block, BF16),
            pltpu.VMEM((2, 4, NX) + block, BF16),
            pltpu.VMEM((2, 4, NX) + block, BF16),
            pltpu.VMEM((NY,) + block, BF16),
            pltpu.VMEM(block, BF16),
            pltpu.VMEM((NF, HD, ROWS), BF16),
            pltpu.VMEM((NF, HD, ROWS), BF16),
            pltpu.VMEM((NF, HD, ROWS), BF16),
            pltpu.VMEM((NF * HD, NF * HD), F32),
            pltpu.VMEM(block, BF16),
            pltpu.VMEM((FAR + 1, HD, TILE), BF16),
            pltpu.VMEM((BAND,) + block, F32),
            pltpu.VMEM((16, NB), jnp.int32),
            pltpu.SMEM((16, NB), jnp.int32),
            pltpu.VMEM((2, 8, 16, 128), F32),
            pltpu.VMEM((8, 16, 128), F32),
            pltpu.VMEM((8, 16, 128), F32),
            pltpu.VMEM((7, 16, 128), F32),
            pltpu.VMEM((8, 16, 128), F32),
            pltpu.VMEM((8, 16, 128), F32),
            pltpu.VMEM((8, 16, 128), F32),
            dma(6), dma(2), dma(2),
            dma(2, 4, 4), dma(2, 4, 4), dma(2, 4, 4), dma(2, 4, 4),
            dma(2, 8, 2), dma(2, 8, 2), dma(2, 8, 2), dma(2, 8, 2), one, one,
            dma(3, 3), dma(3, 3), dma(16), dma(16),
            dma(16, 2), dma(16, 2), dma(16, 2), dma(16, 2),
            dma(2, 4, 4), dma(2, 4, 4), dma(2, 4, 4), dma(2, 4, 4),
            dma(2), dma(2), dma(7), dma(7), dma(7), dma(7), dma(7), dma(7),
        ],
        compiler_params=pltpu.CompilerParams(
            collective_id=0, has_side_effects=True, vmem_limit_bytes=60 * 2**20
        ),
    )(features, near, far_tiles, source, index, source, index, weight.T, bias[None, :], grad_out)
    return act, gfeat, gw.T, gb[0]


def solution(mesh):
    return jax.shard_map(
        on_device,
        mesh=mesh,
        in_specs=(
            P("feat", "blk"),
            P("blk", None, None),
            P("blk", None, None),
            P("blk", None),
            P("blk", None),
            P(None, "feat"),
            P("feat"),
            P("feat", "blk"),
        ),
        out_specs=(P("feat", "blk"), P("feat", "blk"), P(None, "feat"), P("feat")),
        check_vma=False,
    )
```

time: 1720 us -> 101 us (0.06)
  waiting for transfers between devices: 1000 us -> 0 us
  blocking collectives: 492 us -> 0 us
  starting transfers between devices: 109 us -> 0 us
  Pallas kernels: 0 us -> 95.1 us
  local copies, waits for them, and re-layouts: 57.3 us -> 5.4 us
  other arithmetic: 19.9 us -> 0 us
  matrix products: 17.6 us -> 0 us
    psum x1 -> x0, waiting for transfers between devices: 894 us -> none  [on_device(): grad_weight, grad_bias = lax.psum((weight_part, bias_part), 'blk')]
    psum x1 -> x0, blocking collectives: 479 us -> none  [on_device(): grad_weight, grad_bias = lax.psum((weight_part, bias_part), 'blk')]
    pallas_call x0 -> x1, Pallas kernels: none -> 95.1 us  [on_device(): pl.pallas_call(kernel, out_shape=(jax.ShapeDtypeStruct((HD, ROWS), BF16),...]
    ppermute x12 -> x0, waiting for transfers between devices: 72.4 us -> none  [shifted(): return lax.ppermute(block, axis, route)]
    ppermute x12 -> x0, starting transfers between devices: 64.8 us -> none  [shifted(): return lax.ppermute(block, axis, route)]
    all_to_all x3 -> x0, starting transfers between devices: 44.4 us -> none  [the longest x1 20.9 us: on_device(): lax.all_to_all(requests, 'blk', split_axis=0, concat_axis=0, tiled=True)]
    reduce_scatter x1 -> x0, waiting for transfers between devices: 24.3 us -> none  [on_device(): lax.psum_scatter(jnp.dot(weight, grad_pre, preferred_element_type=jnp.flo...]
    dot_general x8 -> x0, matrix products: 17.6 us -> none  [the longest x1 5.28 us: on_device(): jnp.einsum('khb,kab->kha', far_inputs, far_tiles, preferred_element_type=...]
  transfers between devices with their start and end apart: 17 -> 0, of which waited for: 4 -> 0; matrix products, arithmetic and copies ran while one was open for 1% -> 0% of each run, Pallas kernels for 0% -> 0%
where the time goes in v2:
time: 101 us
  Pallas kernels  95.1 us (94%)
  local copies, waits for them, and re-layouts  5.4 us (5%)
    pallas_call x1, Pallas kernels, on_device(): pl.pallas_call(kernel, out_shape=(jax.ShapeDtypeStruct((HD, ROWS), BF16),...  95.1 us
    unnamed x4, local copies, waits for them, and re-layouts  5.4 us

profile of v2, /device:TPU:1, one launch (start us, length us, event | category | flops | bytes accessed | tf_op | source)
XLA Modules:
  0.0 101.2 jit_solution(1417280309437150374)
XLA Ops:
  0.6 95.1 %shard_map.111 = (bf16[64,256]{1,0:T(8,128)(2,1)}, bf16[64,256]{1,0:T(8,128)(2,1)}, f32[64,256]{1,0:T(8,128)}, f32[1,64]{1,0:T(1,128)}) custom-call(bf16[64,256]{1,0:T(8,128)(2,1)} %feat_hbm.1, bf16[7,256,256]{2,1,0:T(8,128)(2,1)} %bitcast.7, bf16[96,128,128]{2,1,0:T(8,128)(2,1)} %far_hbm.1, s32[1,96]{1,0:T(1,128)} %bitcast.12, s32[2,96]{1,0:T(2,128)} %bitcast.10, ...), custom_call_target="tpu_custom_call" | custom-call | tf_op jit(solution)/shard_map/pallas_call | solution.py:723
  95.8 1.4 %copy.16 = bf16[64,256]{1,0:T(8,128)(2,1)} copy(bf16[64,256]{1,0:T(8,128)(2,1)} %get-tuple-element.16) | data formatting | bytes 65536
  97.1 1.4 %copy.17 = bf16[64,256]{1,0:T(8,128)(2,1)} copy(bf16[64,256]{1,0:T(8,128)(2,1)} %get-tuple-element.17) | data formatting | bytes 65536
  98.5 1.5 %copy.18 = f32[256,64]{0,1:T(8,128)} copy(f32[256,64]{0,1:T(8,128)} %bitcast.8) | data formatting | bytes 131072
  100.0 1.2 %copy.19 = f32[64]{0:T(128)} copy(f32[64]{0:T(128)} %bitcast.15) | data formatting | bytes 512

commit v3 on v2

--- a/solution.py
+++ b/solution.py
@@ -48,7 +48,7 @@
     return (c % 2) * HALF + ((c // 4) % 8) * GROUP + ((c // 2) % 2) * NX + c // 32
 
 
-def gather_blocks(X, me, sy, ry, sR, rR, sL, rL, sXR, rXR, sXL, rXL, sP, rP):
+def gather_blocks(X, me, share, sy, ry, sR, rR, sL, rL, sXR, rXR, sXL, rXL, sP, rP):
     x, z, y, core, at = me
     east, west = at(rem(x + 1, NX), z, y, core), at(rem(x + NX - 1, NX), z, y, core)
     partner, across = at(x, z, y, 1 - core), at(x, z, 1 - y, core)
@@ -171,6 +171,7 @@
         got(0, 0)
         swapped()
         ring_start(0, x, 0, 1, True)
+        share()
         hop(0, 1, 0)
         hop(0, 0, 1)
         got(2, 0)
@@ -230,6 +231,7 @@
         for copy in across_x(1):
             copy.start()
         ring_start(1, x, 0, 1, False)
+        share()
         second(0, (1, 3, 2))
         along(0, 0)
         third(0, (0,))
@@ -276,11 +278,7 @@
 
 
 def to_feat(S, f, sent, got):
-    copies = []
-    for d in (1, 2, 3):
-        copies.append(send(S.at[f], S.at[f], sent.at[d - 1], got.at[d - 1], feat=rem(f + d, NF)))
-        copies[-1].start()
-    return copies
+    return [send(S.at[f], S.at[f], sent.at[d - 1], got.at[d - 1], feat=rem(f + d, NF)) for d in (1, 2, 3)]
 
 
 def from_feat(S, f, sent, got):
@@ -405,7 +403,7 @@
             copy.wait_recv()
         return x_total(7, w) + XE[14 + w, 0].astype(F32)
 
-    order = tuple((j, w) for w in range(2) for j in range(8))
+    order = tuple((j, w) for j in range(8) for w in range(2))
     last = send(Fs.at[0], Fr, sy, ry, blk=across)
 
     def deliver(w, total):
@@ -444,9 +442,8 @@
                 if j == 7:
                     for copy in across_x(w):
                         copy.start()
-                if (j, w) == (4, 1):
+                if (j, w) == (7, 1):
                     deliver(0, from_x(0))
-                if (j, w) == (7, 1):
                     deliver(1, from_x(1))
                 if n in hooks:
                     hooks[n]()
@@ -485,7 +482,7 @@
 def kernel(
     feat_hbm, near_hbm, far_hbm, source_ref, index_ref, source_row, index_row, weight_hbm, bias_ref, gout_hbm,
     act_ref, gfeat_ref, gw_ref, gb_ref,
-    near, far, feat_in, gout_in, X, G, H, XE, XW, RR, RL, Fs, Fr, A, GP, WR, WT, ga, parts, band, rows_v, table,
+    near, far, feat_in, X, G, H, XE, XW, RR, RL, Fs, Fr, A, GP, WR, WT, GO, BI, BC, ga, parts, band, rows_v, table,
     W0, W1, W2, W3, W5, W7, W8,
     local, sy, ry, sR, rR, sL, rL, sXR, rXR, sXL, rXL, sP, rP,
     sf, rf, sH, rH, tXR, uXR, tXL, uXL, tR, uR, tL, uL, sw, rw, sz, rz, sq, rq, sz2, rz2,
@@ -517,11 +514,58 @@
 
     load_feat = pltpu.make_async_copy(feat_hbm, feat_in, local.at[0])
     load_weight = pltpu.make_async_copy(weight_hbm, WR.at[f], local.at[1])
-    load_gout = pltpu.make_async_copy(gout_hbm, gout_in, local.at[2])
+    load_gout = pltpu.make_async_copy(gout_hbm, GO.at[f], local.at[2])
     load_near = pltpu.make_async_copy(near_hbm, near, local.at[3])
     load_far = pltpu.make_async_copy(far_hbm, far, local.at[4])
     for load in (load_feat, load_weight, load_gout, load_near, load_far):
         load.start()
+
+    BI[f] = jnp.broadcast_to(jnp.concatenate([bias_ref[...], bias_ref[...]], axis=1), (8, 2 * HD))
+    load_feat.wait()
+    own = core * HALF + z * GROUP + y * NX + x
+    X[own, 0] = feat_in[:, 0:TILE]
+    X[own, 1] = feat_in[:, TILE:]
+    pl.semaphore_wait(barrier, 18)
+
+    load_weight.wait()
+    load_gout.wait()
+
+    def share():
+        for n, S in ((0, WR), (2, GO), (3, BI)):
+            for copy in to_feat(S, f, sf.at[n], rf.at[n]):
+                copy.start()
+
+    gathered_all = gather_blocks(X, me, share, sy.at[0], ry.at[0], sR, rR, sL, rL, sXR, rXR, sXL, rXL, sP, rP)
+
+    load_near.wait()
+    load_far.wait()
+    total = jnp.zeros((HD, ROWS), F32)
+    for s in range(BAND):
+        spot = spot_of(rem(b + NB + s - 3, NB))
+        total += dot(jnp.concatenate([X[spot, 0], X[spot, 1]], axis=1), near[s], NT)
+
+    def far_forward(n, sums):
+        low, high = sums
+        for r in range(8):
+            q = n * 8 + r
+            value = dot(X[within(spot_of(source_ref[0, q]), NB - 1), within(index_ref[1, q], 1)], far[q], NT)
+            first = index_ref[0, q] == 0
+            low += jnp.where(first, value, 0.0)
+            high += jnp.where(first, 0.0, value)
+        return low, high
+
+    zero = jnp.zeros((HD, TILE), F32)
+    low, high = lax.fori_loop(0, FAR // 8, far_forward, (zero, zero))
+    A[f] = (total + jnp.concatenate([low, high], axis=1)).astype(BF16)
+    for copy in to_feat(A, f, sf.at[1], rf.at[1]):
+        copy.start()
+    for n, S in ((0, WR), (2, GO), (3, BI)):
+        from_feat(S, f, sf.at[n], rf.at[n])
+    WT[...] = jnp.transpose(WR[...].reshape(NF * HD, NF * HD).astype(F32))
+    for n in range(NF):
+        column = jnp.transpose(jnp.broadcast_to(BI[n, 0:1, :], (2 * HD, 2 * HD)))[0:HD]
+        BC[n, :, 0:TILE] = column
+        BC[n, :, TILE:] = column
 
     places = jnp.broadcast_to(spot_of(source_row[...]), (NB, FAR))
     keys = jnp.broadcast_to((lax.broadcasted_iota(jnp.int32, (1, FAR), 1) * 2 + index_row[1:2, :]).astype(F32), (NB, FAR))
@@ -533,51 +577,15 @@
     rows_v[8:16] = jnp.transpose(jnp.broadcast_to(two, (NB, NB)))[0:8].astype(jnp.int32)
     load_table = pltpu.make_async_copy(rows_v, table, local.at[5])
     load_table.start()
-    bias = jnp.transpose(jnp.broadcast_to(jnp.concatenate([bias_ref[...], bias_ref[...]], axis=1), (2 * HD, 2 * HD)))[0:HD]
-    bias = jnp.concatenate([bias, bias], axis=1)
-
-    load_feat.wait()
-    own = core * HALF + z * GROUP + y * NX + x
-    X[own, 0] = feat_in[:, 0:TILE]
-    X[own, 1] = feat_in[:, TILE:]
-    pl.semaphore_wait(barrier, 18)
-
-    gathered_all = gather_blocks(X, me, sy.at[0], ry.at[0], sR, rR, sL, rL, sXR, rXR, sXL, rXL, sP, rP)
-
-    load_weight.wait()
-    zero_th = to_feat(WR, f, sf.at[0], rf.at[0])
-    load_near.wait()
-    load_far.wait()
-    total = jnp.zeros((HD, ROWS), F32)
-    for s in range(BAND):
-        spot = spot_of(rem(b + NB + s - 3, NB))
-        total += dot(jnp.concatenate([X[spot, 0], X[spot, 1]], axis=1), near[s], NT)
-
-    def far_forward(n, sums):
-        low, high = sums
-        for r in range(8):
-            q = n * 8 + r
-            value = dot(X[within(spot_of(source_ref[0, q]), NB - 1), within(index_ref[1, q], 1)], far[q], NT)
-            first = index_ref[0, q] == 0
-            low += jnp.where(first, value, 0.0)
-            high += jnp.where(first, 0.0, value)
-        return low, high
-
-    zero = jnp.zeros((HD, TILE), F32)
-    low, high = lax.fori_loop(0, FAR // 8, far_forward, (zero, zero))
-    A[f] = (total + jnp.concatenate([low, high], axis=1)).astype(BF16)
-    first = to_feat(A, f, sf.at[1], rf.at[1])
-    from_feat(WR, f, sf.at[0], rf.at[0])
-    WT[...] = jnp.transpose(WR[...].reshape(NF * HD, NF * HD).astype(F32))
-    load_gout.wait()
     from_feat(A, f, sf.at[1], rf.at[1])
 
     gathered = A[...].reshape(NF * HD, ROWS)
-    pre = dot(WR[f], gathered, NN) + bias
+    pre = dot(WR[...].reshape(NF * HD, NF * HD), gathered, NN) + BC[...].reshape(NF * HD, ROWS)
     sig = jax.nn.sigmoid(pre)
-    grad_pre = (gout_in[...].astype(F32) * sig * (1.0 + pre * (1.0 - sig))).astype(BF16)
-    GP[f] = grad_pre
-    second = to_feat(GP, f, sf.at[2], rf.at[2])
+    upstream = GO[...].reshape(NF * HD, ROWS).astype(F32)
+    every_grad_pre = (upstream * sig * (1.0 + pre * (1.0 - sig))).astype(BF16)
+    GP[...] = every_grad_pre.reshape(NF, HD, ROWS)
+    grad_pre = GP[f]
     part = dot(grad_pre, gathered, NT)
     ones = dot(jnp.ones((8, ROWS), BF16), grad_pre, NT)
     side = jnp.concatenate([ones, ones], axis=1)
@@ -587,12 +595,12 @@
             W0[k, n, 8:16, :] = side
     halves = send(W0.at[1 - core], W1, sw.at[0], rw.at[0], blk=partner)
     halves.start()
-    act_ref[...] = (pre * sig).astype(BF16)
-    from_feat(GP, f, sf.at[2], rf.at[2])
     own_rows = WT[pl.ds(pl.multiple_of(f * HD, HD), HD), :].astype(BF16)
-    grad = dot(own_rows, GP[...].reshape(NF * HD, ROWS), NN).astype(BF16)
+    grad = dot(own_rows, every_grad_pre, NN).astype(BF16)
     ga[0] = grad[:, 0:TILE]
     ga[1] = grad[:, TILE:]
+    pre = dot(WR[f], gathered, NN) + BC[f]
+    act_ref[...] = jax.nn.silu(pre).astype(BF16)
 
     halves.wait_recv()
     W2[...] = W0[core] + W1[...]
@@ -677,9 +685,10 @@
         zz, yy = group(j, w)
         given(zz, yy, j * 2 + w).start()
 
-    def fill_and_give(w, j, _):
-        fill(j, w)
-        give(j, w)
+    def fill_and_give(j, _):
+        for w in (0, 1):
+            fill(j, w)
+            give(j, w)
         return 0
 
     def fill_near(j, _):
@@ -688,15 +697,13 @@
         return 0
 
     load_table.wait()
-    lax.fori_loop(0, 5, functools.partial(fill_and_give, 0), 0)
+    lax.fori_loop(0, 5, fill_and_give, 0)
     lax.fori_loop(5, 8, fill_near, 0)
     for s in range(BAND):
         spot = spot_of(rem(b + NB + s - 3, NB))
         G[spot] = (G[spot].astype(F32) + band[s]).astype(BF16)
     for j in (5, 6, 7):
         give(j, 0)
-    lax.fori_loop(0, 5, functools.partial(fill_and_give, 1), 0)
-    for j in (5, 6, 7):
         give(j, 1)
 
     run()
@@ -709,7 +716,10 @@
     gathered_all()
     sent()
     halves.wait_send()
-    for copy in zero_th + first + second + to_z + to_slab + again + [final]:
+    for n, S in enumerate((WR, A, GO, BI)):
+        for copy in to_feat(S, f, sf.at[n], rf.at[n]):
+            copy.wait_send()
+    for copy in to_z + to_slab + again + [final]:
         copy.wait_send()
 
 
@@ -734,7 +744,6 @@
             pltpu.VMEM((BAND, ROWS, ROWS), BF16),
             pltpu.VMEM((FAR, TILE, TILE), BF16),
             pltpu.VMEM((HD, ROWS), BF16),
-            pltpu.VMEM((HD, ROWS), BF16),
             pltpu.VMEM((NB,) + block, BF16),
             pltpu.VMEM((NB,) + block, BF16),
             pltpu.VMEM((HALF,) + block, BF16),
@@ -748,6 +757,9 @@
             pltpu.VMEM((NF, HD, ROWS), BF16),
             pltpu.VMEM((NF, HD, ROWS), BF16),
             pltpu.VMEM((NF * HD, NF * HD), F32),
+            pltpu.VMEM((NF, HD, ROWS), BF16),
+            pltpu.VMEM((NF, 8, 2 * HD), F32),
+            pltpu.VMEM((NF, HD, ROWS), F32),
             pltpu.VMEM(block, BF16),
             pltpu.VMEM((FAR + 1, HD, TILE), BF16),
             pltpu.VMEM((BAND,) + block, F32),
@@ -763,7 +775,7 @@
             dma(6), dma(2), dma(2),
             dma(2, 4, 4), dma(2, 4, 4), dma(2, 4, 4), dma(2, 4, 4),
             dma(2, 8, 2), dma(2, 8, 2), dma(2, 8, 2), dma(2, 8, 2), one, one,
-            dma(3, 3), dma(3, 3), dma(16), dma(16),
+            dma(4, 3), dma(4, 3), dma(16), dma(16),
             dma(16, 2), dma(16, 2), dma(16, 2), dma(16, 2),
             dma(2, 4, 4), dma(2, 4, 4), dma(2, 4, 4), dma(2, 4, 4),
             dma(2), dma(2), dma(7), dma(7), dma(7), dma(7), dma(7), dma(7),

time: 101 us -> 94.1 us (0.932)
  Pallas kernels: 95.1 us -> 87.8 us
    pallas_call x1, Pallas kernels: 95.1 us -> 87.8 us  [on_device(): pl.pallas_call(kernel, out_shape=(jax.ShapeDtypeStruct((HD, ROWS), BF16),...]
where the time goes in v3:
time: 94.1 us; the launch traced here: 93.8 us
  Pallas kernels  87.8 us (93%)
  local copies, waits for them, and re-layouts  5.4 us (6%)
    pallas_call x1, Pallas kernels, on_device(): pl.pallas_call(kernel, out_shape=(jax.ShapeDtypeStruct((HD, ROWS), BF16),...  87.8 us
    unnamed x4, local copies, waits for them, and re-layouts  5.4 us

profile of v3, /device:TPU:1, one launch (start us, length us, event | category | flops | bytes accessed | tf_op | source)
XLA Modules:
  0.0 93.8 jit_solution(6776745074912340864)
XLA Ops:
  0.6 87.8 %shard_map.111 = (bf16[64,256]{1,0:T(8,128)(2,1)}, bf16[64,256]{1,0:T(8,128)(2,1)}, f32[64,256]{1,0:T(8,128)}, f32[1,64]{1,0:T(1,128)}) custom-call(bf16[64,256]{1,0:T(8,128)(2,1)} %feat_hbm.1, bf16[7,256,256]{2,1,0:T(8,128)(2,1)} %bitcast.7, bf16[96,128,128]{2,1,0:T(8,128)(2,1)} %far_hbm.1, s32[1,96]{1,0:T(1,128)} %bitcast.12, s32[2,96]{1,0:T(2,128)} %bitcast.10, ...), custom_call_target="tpu_custom_call" | custom-call | tf_op jit(solution)/shard_map/pallas_call | solution.py:733
  88.4 1.4 %copy.16 = bf16[64,256]{1,0:T(8,128)(2,1)} copy(bf16[64,256]{1,0:T(8,128)(2,1)} %get-tuple-element.16) | data formatting | bytes 65536
  89.8 1.4 %copy.17 = bf16[64,256]{1,0:T(8,128)(2,1)} copy(bf16[64,256]{1,0:T(8,128)(2,1)} %get-tuple-element.17) | data formatting | bytes 65536
  91.1 1.5 %copy.18 = f32[256,64]{0,1:T(8,128)} copy(f32[256,64]{0,1:T(8,128)} %bitcast.8) | data formatting | bytes 131072
  92.6 1.2 %copy.19 = f32[64]{0:T(128)} copy(f32[64]{0:T(128)} %bitcast.15) | data formatting | bytes 512

commit v4 on v3

--- a/solution.py
+++ b/solution.py
@@ -403,7 +403,7 @@
             copy.wait_recv()
         return x_total(7, w) + XE[14 + w, 0].astype(F32)
 
-    order = tuple((j, w) for j in range(8) for w in range(2))
+    order = ((0, 0),) + tuple(o for j in range(1, 8) for o in ((j, 0), (j - 1, 1))) + ((7, 1),)
     last = send(Fs.at[0], Fr, sy, ry, blk=across)
 
     def deliver(w, total):

time: 94.1 us -> 92.1 us (0.979)
  Pallas kernels: 87.8 us -> 85.7 us
    pallas_call x1, Pallas kernels: 87.8 us -> 85.7 us  [on_device(): pl.pallas_call(kernel, out_shape=(jax.ShapeDtypeStruct((HD, ROWS), BF16),...]
where the time goes in v4:
time: 92.1 us; the launch traced here: 91.7 us
  Pallas kernels  85.7 us (93%)
  local copies, waits for them, and re-layouts  5.4 us (6%)
    pallas_call x1, Pallas kernels, on_device(): pl.pallas_call(kernel, out_shape=(jax.ShapeDtypeStruct((HD, ROWS), BF16),...  85.7 us
    unnamed x4, local copies, waits for them, and re-layouts  5.4 us

profile of v4, /device:TPU:1, one launch (start us, length us, event | category | flops | bytes accessed | tf_op | source)
XLA Modules:
  0.0 91.7 jit_solution(8214545227237474380)
XLA Ops:
  0.6 85.7 %shard_map.111 = (bf16[64,256]{1,0:T(8,128)(2,1)}, bf16[64,256]{1,0:T(8,128)(2,1)}, f32[64,256]{1,0:T(8,128)}, f32[1,64]{1,0:T(1,128)}) custom-call(bf16[64,256]{1,0:T(8,128)(2,1)} %feat_hbm.1, bf16[7,256,256]{2,1,0:T(8,128)(2,1)} %bitcast.7, bf16[96,128,128]{2,1,0:T(8,128)(2,1)} %far_hbm.1, s32[1,96]{1,0:T(1,128)} %bitcast.12, s32[2,96]{1,0:T(2,128)} %bitcast.10, ...), custom_call_target="tpu_custom_call" | custom-call | tf_op jit(solution)/shard_map/pallas_call | solution.py:733
  86.3 1.4 %copy.16 = bf16[64,256]{1,0:T(8,128)(2,1)} copy(bf16[64,256]{1,0:T(8,128)(2,1)} %get-tuple-element.16) | data formatting | bytes 65536
  87.7 1.4 %copy.17 = bf16[64,256]{1,0:T(8,128)(2,1)} copy(bf16[64,256]{1,0:T(8,128)(2,1)} %get-tuple-element.17) | data formatting | bytes 65536
  89.1 1.5 %copy.18 = f32[256,64]{0,1:T(8,128)} copy(f32[256,64]{0,1:T(8,128)} %bitcast.8) | data formatting | bytes 131072
  90.5 1.2 %copy.19 = f32[64]{0:T(128)} copy(f32[64]{0:T(128)} %bitcast.15) | data formatting | bytes 512
